TPU v7x, 32 devices: a whole 2x2x4 slice. The times are simulated.
32 devices in a mesh: row: 8 (over z, y), col: 4 (over x, core).
Axes of the slice: x: 2, y: 2, z: 4, core: 2. Of those that a mesh axis runs over, the one named last changes fastest.
Arguments:
- x_tiles: bfloat16 [192, 512, 128], P('row', 'col'), may hold values from -1.328125 to 1.328125
- tile_pos: int32 [8, 96], P('row', 'col'), may hold values from 0 to 127, as said below
- panel_ids: int32 [4], replicated, may hold values from 0 to 15, as said below
Outputs:
- square_part: float32 [8192, 8192], P('row', 'col')
Inputs may be any that keep to these rules, and one draw needn't show every extreme that they name: `tile_pos`: on each device the 24 positions are distinct and increasing. Split the device's 8 x 16 local blocks into squares of 4 x 4 blocks aligned to multiples of 4: one square (drawn) holds exactly 10 stored blocks and every other square exactly 2. `panel_ids`: the 4 panels are distinct, and one of them is the last panel.
All inputs are finite; a program needn't handle non-finite values.
Results may differ from a plain program's by a relative error of at most 0.0003.
Values may be sent and summed in bfloat16 or wider, within the bound.
No kernel may reach another device: no remote copies, remote signals or barrier semaphores. Data moves between devices by JAX's collectives and lax.ppermute only.
A program may use at most 64 MiB of HBM per device.

v0:
```python
import jax
import jax.numpy as jnp
from jax import lax
from jax.sharding import PartitionSpec as P

LR = 8
PW = 4
SECTIONS = 4


def spread(shard, axis, root):
    mine = lax.axis_index(axis) == root
    return lax.psum(jnp.where(mine, shard, jnp.zeros_like(shard)), axis)


def per_device(x_tiles, tile_pos, panel_ids):
    blocksz = x_tiles.shape[1]
    col_count = LR * lax.axis_size("row") // lax.axis_size("col")
    positions = tile_pos[0]
    local_rows = positions // col_count
    local_cols = positions % col_count
    grid = (
        jnp.zeros((LR, col_count, blocksz, blocksz), x_tiles.dtype)
        .at[local_rows, local_cols]
        .set(x_tiles)
    )
    dense = grid.transpose(0, 2, 1, 3).reshape(LR * blocksz, col_count * blocksz)
    result = jnp.zeros((LR * blocksz, col_count * blocksz), jnp.float32)
    for section in range(SECTIONS):
        first = panel_ids[section] * PW
        owner_col = first // col_count
        col_offset = first - owner_col * col_count
        owner_row = first // LR
        row_offset = first - owner_row * LR
        column_piece = lax.dynamic_slice_in_dim(dense, col_offset * blocksz, PW * blocksz, 1)
        column_panel = spread(column_piece, "col", owner_col)
        row_piece = lax.dynamic_slice_in_dim(dense, row_offset * blocksz, PW * blocksz, 0)
        row_panel = spread(row_piece, "row", owner_row)
        result = result + jnp.dot(column_panel, row_panel, preferred_element_type=jnp.float32)
    return result


def solution(mesh):
    in_specs = (P("row", "col", None), P("row", "col"), P())
    out_specs = P("row", "col")
    return jax.shard_map(
        per_device, mesh=mesh, in_specs=in_specs, out_specs=out_specs, check_vma=False
    )
```

profile of v0, /device:TPU:0, one launch (start us, length us, event | category | flops | bytes accessed | tf_op | source)
XLA Modules:
  0.0 429.1 jit_solution(18136810767104236946)
XLA Ops:
  6.5 0.0 all-reduce.7.cloned.1.call-start
  6.5 1.4 fusion.2
  10.6 0.7 fusion.1
  11.2 0.0 copy-start.1
  11.2 3.1 broadcast_in_dim.2
  14.3 0.0 copy-done.1
  14.3 4.9 %scatter_fusion = bf16[8,16,128,128]{3,2,1,0:T(8,128)(2,1)} fusion(bf16[8,16,128,128]{3,2,1,0:T(8,128)(2,1)} %broadcast_in_dim.2, s32[24]{0:T(128)S(1)} %fusion.1, bf16[24,128,128]{2,1,0:T(8,128)(2,1)S(1)} %copy-done.1), kind=kCustom, calls=%fused_computation | custom fusion | bytes 2359488 | tf_op jit(solution)/shard_map/scatter | solution.py:25
  19.2 4.9 %copy.4 = bf16[8,128,16,128]{3,2,1,0:T(8,128)(2,1)S(1)} copy(bf16[8,128,16,128]{3,1,2,0:T(8,128)(2,1)} %bitcast.38) | data formatting | bytes 8388608 | tf_op jit(solution)/shard_map/transpose | solution.py:27
  24.1 4.1 copy.7
  28.2 4.7 %dynamic-slice_select_fusion.4 = (bf16[1024,512]{1,0:T(8,128)(2,1)}, bf16[1024,512]{1,0:T(8,128)(2,1)}, bf16[1024,512]{1,0:T(8,128)(2,1)}, bf16[1024,512]{1,0:T(8,128)(2,1)}) fusion(bf16[1024,2048]{1,0:T(8,128)(2,1)} %bitcast.36, s32[]{:T(128)S(6)} %select_n.177, pred[]{:T(512)S(6)} %eq.32, s32[]{:T(128)S(6)} %select_n.169, pred[]{:T(512)S(6)} %eq.30, ...), kind=kLoop, calls=%fused_computation.7 | loop fusion | flops 2097152 | bytes 8388628 | tf_op jit(solution)/shard_map/jit(_where)/select_n | solution.py:13
  32.9 0.0 all-reduce.7.cloned.1.call-update
  32.9 0.2 all-reduce.5.cloned.1.call-start
  33.3 9.0 %dynamic-slice_select_fusion = (bf16[512,2048]{1,0:T(8,128)(2,1)}, bf16[512,2048]{1,0:T(8,128)(2,1)}, bf16[512,2048]{1,0:T(8,128)(2,1)}, bf16[512,2048]{1,0:T(8,128)(2,1)}) fusion(bf16[1024,2048]{1,0:T(8,128)(2,1)} %bitcast.37, s32[]{:T(128)S(6)} %select_n.181, pred[]{:T(512)S(6)} %eq.33, s32[]{:T(128)S(6)} %select_n.173, pred[]{:T(512)S(6)} %eq.31, ...), kind=kLoop, calls=%fused_computation.3 | loop fusion | flops 4194304 | bytes 16777236 | tf_op jit(solution)/shard_map/jit(_where)/select_n | solution.py:13
  42.3 0.0 all-reduce.5.cloned.1.call-update
  42.3 79.5 %all-reduce.7.cloned.1.call-done = (bf16[1024,512]{1,0:T(8,128)(2,1)}, bf16[1024,512]{1,0:T(8,128)(2,1)}, bf16[1024,512]{1,0:T(8,128)(2,1)}, bf16[1024,512]{1,0:T(8,128)(2,1)}) async-done(((bf16[1024,512]{1,0:T(8,128)(2,1)}, bf16[1024,512]{1,0:T(8,128)(2,1)}, bf16[1024,512]{1,0:T(8,128)(2,1)}, bf16[1024,512]{1,0:T(8,128)(2,1)}), (bf16[1024,512]{1,0:T(8,128)(2,1)}, bf16[1024,512]{1,0:T(8,128)(2,1)}, ...) | async-done | bytes 4194320 | tf_op jit(solution)/shard_map/psum | solution.py:13
  121.8 278.0 %all-reduce.5.cloned.1.call-done = (bf16[512,2048]{1,0:T(8,128)(2,1)}, bf16[512,2048]{1,0:T(8,128)(2,1)}, bf16[512,2048]{1,0:T(8,128)(2,1)}, bf16[512,2048]{1,0:T(8,128)(2,1)}) async-done(((bf16[512,2048]{1,0:T(8,128)(2,1)}, bf16[512,2048]{1,0:T(8,128)(2,1)}, bf16[512,2048]{1,0:T(8,128)(2,1)}, bf16[512,2048]{1,0:T(8,128)(2,1)}), (bf16[512,2048]{1,0:T(8,128)(2,1)}, bf16[512,2048]{1,0:T(8,128)(2,1)}, ...) | async-done | bytes 8388624 | tf_op jit(solution)/shard_map/psum | solution.py:13
  399.8 0.0 copy-start.3
  399.8 0.0 copy-start.5
  399.8 4.4 %fusion.5 = f32[1024,2048]{1,0:T(8,128)S(1)} fusion(bf16[1024,512]{1,0:T(8,128)(2,1)} %get-tuple-element.9, bf16[512,2048]{1,0:T(8,128)(2,1)} %get-tuple-element.5), kind=kOutput, calls=%fused_computation.27 | convolution fusion | flops 2147483648 | bytes 11534336 | tf_op jit(solution)/shard_map/dot_general | solution.py:39
  404.2 0.0 copy-done.3
  404.2 0.0 copy-done.5
  404.2 0.0 copy-start.2
  404.2 0.0 copy-start.4
  404.2 2.3 fusion.3
  406.6 0.0 copy-done.2
  406.6 0.0 copy-done.4
  406.6 0.0 copy-start
  406.6 5.7 %fusion.4 = f32[1024,2048]{1,0:T(8,128)} fusion(bf16[1024,512]{1,0:T(8,128)(2,1)S(1)} %copy-done.4, bf16[512,2048]{1,0:T(8,128)(2,1)S(1)} %copy-done.2), kind=kOutput, calls=%fused_computation.26 | convolution fusion | flops 2147483648 | bytes 11534336 | tf_op jit(solution)/shard_map/dot_general | solution.py:39
  412.3 0.0 copy-done
  412.3 9.9 %add_add_fusion = f32[1024,2048]{1,0:T(8,128)} fusion(f32[1024,2048]{1,0:T(8,128)S(1)} %fusion.5, f32[1024,2048]{1,0:T(8,128)S(1)} %fusion.3, f32[1024,2048]{1,0:T(8,128)} %fusion.4, bf16[1024,512]{1,0:T(8,128)(2,1)} %get-tuple-element.12, bf16[512,2048]{1,0:T(8,128)(2,1)S(1)} %copy-done), kind=kOutput, calls=%fused_computation.1 | convolution fusion | flops 2153775104 | bytes 36700160 | tf_op jit(solution)/shard_map/dot_general | solution.py:39
Async XLA Ops:
  6.5 115.3 %all-reduce.7.cloned.1.call-start = ((), (), s32[]{:S(2)}) async-start(), calls=%async_computation.1 | async-start | bytes 8388608 | tf_op jit(solution)/shard_map/psum | solution.py:13
  11.2 3.1 copy-start.1
  32.9 366.9 %all-reduce.5.cloned.1.call-start = ((), (), s32[]{:S(2)}) async-start(), calls=%async_computation | async-start | bytes 16777216 | tf_op jit(solution)/shard_map/psum | solution.py:13
  399.8 4.4 %copy-start.3 = (bf16[512,2048]{1,0:T(8,128)(2,1)S(1)}, bf16[512,2048]{1,0:T(8,128)(2,1)}, u32[]{:S(2)}) copy-start(bf16[512,2048]{1,0:T(8,128)(2,1)} %get-tuple-element.6) | copy-start | bytes 6291460
  399.8 4.4 %copy-start.5 = (bf16[1024,512]{1,0:T(8,128)(2,1)S(1)}, bf16[1024,512]{1,0:T(8,128)(2,1)}, u32[]{:S(2)}) copy-start(bf16[1024,512]{1,0:T(8,128)(2,1)} %get-tuple-element.10) | copy-start | bytes 3145732
  404.2 2.4 copy-start.2
  404.2 2.4 copy-start.4
  406.6 5.8 %copy-start = (bf16[512,2048]{1,0:T(8,128)(2,1)S(1)}, bf16[512,2048]{1,0:T(8,128)(2,1)}, u32[]{:S(2)}) copy-start(bf16[512,2048]{1,0:T(8,128)(2,1)} %get-tuple-element.8) | copy-start | bytes 6291460
Sparse Core Ops, SparseCore 0:
  33.0 88.7 all-reduce.6
  127.1 272.6 all-reduce.4
where the time goes:
time: 430 us; the launch traced here: 429 us
  waiting for transfers between devices  357 us (83%)
  matrix products  22.4 us (5%)
  local copies, waits for them, and re-layouts  18.4 us (4%)
  between operations  16.2 us (4%)
  other arithmetic  14.4 us (3%)
    psum x2, waiting for transfers between devices, spread(): return lax.psum(jnp.where(mine, shard, jnp.zeros_like(shard)), axis)  357 us
    dot_general x4, matrix products, per_device(): jnp.dot(column_panel, row_panel, preferred_element_type=jnp.float32)  22.4 us
    select_n x2, other arithmetic, spread(): return lax.psum(jnp.where(mine, shard, jnp.zeros_like(shard)), axis)  13.7 us
  transfers between devices with their start and end apart: 2, of which 2 were waited for; matrix products, arithmetic and copies ran while one was open for 2% of the time, Pallas kernels for 0%

commit v1 on v0

v1 whole, which is shorter than its diff:
```python
import functools

import jax
import jax.numpy as jnp
from jax import lax
from jax.experimental import pallas as pl
from jax.experimental.pallas import tpu as pltpu
from jax.sharding import PartitionSpec as P

LR = 8
PW = 4
SECTIONS = 4
QD = 10
QS = 2
NOTE = 16
AT_ONCE = 4


class Sizes:
    def __init__(self, rows, cols, slots, bs):
        self.rows, self.cols, self.slots, self.bs = rows, cols, slots, bs
        self.lc = LR * rows // cols
        panel_most = (self.lc // PW) * QS + (QD - QS)
        self.share = -(-panel_most // rows)
        self.near = -(-max(0, slots - rows * self.share) // self.share)
        self.held = SECTIONS * self.share
        self.depth = SECTIONS * PW

    def given(self, d):
        return self.share * (2 if d < self.near else 1)


def section_of(panels_ref, panel):
    found = jnp.int32(-1)
    for j in range(SECTIONS):
        found = jnp.where(panels_ref[j] == panel, jnp.int32(j), found)
    return found


def owned_by(panels_ref, row):
    count, first, last = jnp.int32(0), jnp.int32(-1), jnp.int32(0)
    for j in reversed(range(SECTIONS)):
        mine = panels_ref[j] // (LR // PW) == row
        last = jnp.where(mine & (count == 0), j, last)
        first = jnp.where(mine, j, first)
        count = count + mine.astype(jnp.int32)
    return count, first, last


def deal(sz, count, picked, e, i):
    i = jnp.where(picked, i + 1, i)
    full = i == jnp.where((count == 2) & (e < sz.near), 2 * sz.share, sz.share)
    return jnp.where(full, e + 1, e), jnp.where(full, 0, i)


def pack_kernel(sz, pos_ref, panels_ref, pos_row_ref, x_ref, *refs):
    outs, all_ref, src_ref = refs[: sz.rows], refs[sz.rows], refs[sz.rows + 1]
    row = lax.axis_index("row")
    count, _, _ = owned_by(panels_ref, row)
    bs, most = sz.bs, 2 * sz.share
    for e in range(sz.rows * most):
        src_ref[e] = 0

    def one(s, state):
        e, i = state
        panel = row * (LR // PW) + pos_ref[0, s] // (sz.lc * PW)
        picked = section_of(panels_ref, panel) >= 0

        @pl.when(picked)
        def _():
            src_ref[e * most + i] = s

        return deal(sz, count, picked, e, i)

    lax.fori_loop(0, sz.slots, one, (jnp.int32(0), jnp.int32(0)))
    note = jnp.broadcast_to(pos_row_ref[...].astype(jnp.float32), (NOTE, sz.slots)).astype(x_ref.dtype)
    for e in range(sz.rows):
        for i in range(sz.given(e)):
            outs[e][i * bs : (i + 1) * bs] = x_ref[src_ref[e * most + i]]
        outs[e][sz.given(e) * bs :, : sz.slots] = note
    for s in range(sz.slots):
        all_ref[s * bs : (s + 1) * bs] = x_ref[s]
    all_ref[sz.slots * bs :, : sz.slots] = note


def hold_kernel(sz, panels_ref, *refs):
    came, hold_ref, notes_ref = refs[: sz.rows], refs[sz.rows], refs[sz.rows + 1]
    row = lax.axis_index("row")
    n = sz.share * sz.bs
    for d in range(sz.rows):
        note = came[d][sz.given(d) * sz.bs :].astype(jnp.float32)[:1, : sz.slots]
        notes_ref[d : d + 1, :] = note.astype(jnp.int32)
    for j in range(SECTIONS):
        owner = panels_ref[j] // (LR // PW)
        _, first, _ = owned_by(panels_ref, owner)
        for d in range(sz.rows):

            @pl.when(((owner ^ row) == d) & (first == j))
            def _():
                hold_ref[j * n : (j + 1) * n] = came[d][:n]

            if d < sz.near:

                @pl.when(((owner ^ row) == d) & (first != j))
                def _():
                    hold_ref[j * n : (j + 1) * n] = came[d][n : 2 * n]


def column_meta_kernel(sz, notes_ref, panels_ref, b_list):
    row = lax.axis_index("row")

    def clear(i, _):
        b_list[i] = -1
        return 0

    lax.fori_loop(0, sz.rows * sz.held, clear, 0)

    def one_row(owner, _):
        count, first, last = owned_by(panels_ref, owner)

        def one(s, state):
            e, i = state
            pos = notes_ref[owner ^ row, s]
            local_row, local_col = pos // sz.lc, pos % sz.lc
            section = section_of(panels_ref, owner * (LR // PW) + local_row // PW)
            picked = section >= 0

            @pl.when(picked)
            def _():
                at = jnp.where(i < sz.share, first * sz.share + i, last * sz.share + i - sz.share)
                b_list[(owner ^ e ^ row) * sz.held + at] = (section * PW + local_row % PW) * sz.lc + local_col

            return deal(sz, count, picked, e, i)

        @pl.when(count > 0)
        def _():
            lax.fori_loop(0, sz.slots, one, (jnp.int32(0), jnp.int32(0)))

        return 0

    lax.fori_loop(0, sz.rows, one_row, 0)


def row_meta_kernel(sz, notes_ref, panels_ref, a_list):
    for i in range(LR):
        a_list[i * (sz.depth + 1)] = 0

    def one(t, _):
        owner, s = t // sz.slots, t % sz.slots
        pos = notes_ref[owner, s]
        local_row, local_col = pos // sz.lc, pos % sz.lc
        section = section_of(panels_ref, owner * (sz.lc // PW) + local_col // PW)

        @pl.when(section >= 0)
        def _():
            base = local_row * (sz.depth + 1)
            n = a_list[base] + 1
            a_list[base + n] = t * sz.depth + section * PW + local_col % PW
            a_list[base] = n

        return 0

    lax.fori_loop(0, sz.cols * sz.slots, one, 0)


def product_kernel(sz, a_list, b_list, a_ref, *refs):
    b_refs = refs[: sz.rows]
    out_ref, lhs, b_dense = refs[sz.rows :]
    bs, depth = sz.bs, sz.depth
    step = pl.program_id(0)

    @pl.when(step == 0)
    def _():
        b_dense[...] = jnp.zeros_like(b_dense)
        for e in range(sz.rows):
            for h in range(sz.held):
                at = b_list[e * sz.held + h]

                @pl.when(at >= 0)
                def _():
                    k, c = at // sz.lc, at % sz.lc
                    b_dense[k, :, pl.ds(pl.multiple_of(c * bs, bs), bs)] = b_refs[e][h * bs : (h + 1) * bs]

    base = step * (depth + 1)
    n = a_list[base]
    width = out_ref.shape[1]
    chunk = min(width, 512)

    def group(g, first):
        ks = []
        for u in range(AT_ONCE):
            t = g * AT_ONCE + u
            there = t < n
            code = jnp.where(there, a_list[base + 1 + jnp.minimum(t, depth - 1)], 0)
            place, k = code // depth, code % depth
            owner, s = place // sz.slots, place % sz.slots
            block = a_ref[owner, pl.ds(pl.multiple_of(s * bs, bs), bs), :]
            lhs[:, u * bs : (u + 1) * bs] = jnp.where(there, block, jnp.zeros_like(block))
            ks.append(k)
        for c in range(0, width, chunk):
            rhs = jnp.concatenate([b_dense[k, :, c : c + chunk] for k in ks], axis=0)
            part = jnp.dot(lhs[...], rhs, preferred_element_type=jnp.float32)
            if first:
                out_ref[:, c : c + chunk] = part
            else:
                out_ref[:, c : c + chunk] += part

    group(0, True)

    def more(g, _):
        group(g, False)
        return 0

    lax.fori_loop(1, (n + AT_ONCE - 1) // AT_ONCE, more, 0)


def flip(x, axis, d):
    return lax.ppermute(x, axis, [(i, i ^ d) for i in range(lax.axis_size(axis))])


def gather_by_flips(x, axis):
    n = lax.axis_size(axis)
    got, bit = {0: x}, n // 2
    while bit:
        for d in list(got):
            got[d | bit] = flip(got[d], axis, bit)
        bit //= 2
    return [got[d] for d in range(n)]


def per_device(x_tiles, tile_pos, panel_ids):
    rows, cols = lax.axis_size("row"), lax.axis_size("col")
    slots, bs, _ = x_tiles.shape
    dtype = x_tiles.dtype
    sz = Sizes(rows, cols, slots, bs)
    smem = pl.BlockSpec(memory_space=pltpu.SMEM)
    vmem = pl.BlockSpec(memory_space=pltpu.VMEM)

    *parts, mine = pl.pallas_call(
        functools.partial(pack_kernel, sz),
        out_shape=[jax.ShapeDtypeStruct((sz.given(d) * bs + NOTE, bs), dtype) for d in range(rows)]
        + [jax.ShapeDtypeStruct((slots * bs + NOTE, bs), dtype)],
        in_specs=[smem, smem, vmem, vmem],
        out_specs=[vmem] * (rows + 1),
        scratch_shapes=[pltpu.SMEM((rows * 2 * sz.share,), jnp.int32)],
    )(tile_pos, panel_ids, tile_pos, x_tiles)

    a_all = lax.all_gather(mine, "col")
    came = [parts[0]] + [flip(parts[d], "row", d) for d in range(1, rows)]
    hold, column_notes = pl.pallas_call(
        functools.partial(hold_kernel, sz),
        out_shape=[
            jax.ShapeDtypeStruct((sz.held * bs, bs), dtype),
            jax.ShapeDtypeStruct((rows, slots), jnp.int32),
        ],
        in_specs=[smem] + [vmem] * rows,
        out_specs=[vmem, vmem],
    )(panel_ids, *came)
    b_parts = gather_by_flips(hold, "row")

    b_list = pl.pallas_call(
        functools.partial(column_meta_kernel, sz),
        out_shape=jax.ShapeDtypeStruct((rows * sz.held,), jnp.int32),
        in_specs=[smem, smem],
        out_specs=smem,
    )(column_notes, panel_ids)
    a_list = pl.pallas_call(
        functools.partial(row_meta_kernel, sz),
        out_shape=jax.ShapeDtypeStruct((LR * (sz.depth + 1),), jnp.int32),
        in_specs=[smem, smem],
        out_specs=smem,
    )(a_all[:, -1, :slots].astype(jnp.int32), panel_ids)

    width = sz.lc * bs
    return pl.pallas_call(
        functools.partial(product_kernel, sz),
        out_shape=jax.ShapeDtypeStruct((LR * bs, width), jnp.float32),
        grid_spec=pltpu.PrefetchScalarGridSpec(
            num_scalar_prefetch=2,
            grid=(LR,),
            in_specs=[pl.BlockSpec((cols, slots * bs + NOTE, bs), lambda i, *_: (0, 0, 0))]
            + [pl.BlockSpec((sz.held * bs, bs), lambda i, *_: (0, 0))] * rows,
            out_specs=pl.BlockSpec((bs, width), lambda i, *_: (i, 0)),
            scratch_shapes=[
                pltpu.VMEM((bs, AT_ONCE * bs), dtype),
                pltpu.VMEM((sz.depth, bs, width), dtype),
            ],
        ),
        compiler_params=pltpu.CompilerParams(vmem_limit_bytes=40 * 2**20),
        cost_estimate=pl.CostEstimate(flops=2 * 10**9, bytes_accessed=12 * 2**20, transcendentals=0),
    )(a_list, b_list, a_all, *b_parts)


def solution(mesh):
    in_specs = (P("row", "col", None), P("row", "col"), P())
    out_specs = P("row", "col")
    return jax.shard_map(
        per_device, mesh=mesh, in_specs=in_specs, out_specs=out_specs, check_vma=False
    )
```

time: 430 us -> 91.1 us (0.21)
  waiting for transfers between devices: 357 us -> 23.3 us
  starting transfers between devices: 0.22 us -> 24.5 us
  Pallas kernels: 0 us -> 23.3 us
  matrix products: 22.4 us -> 0 us
  local copies, waits for them, and re-layouts: 18.4 us -> 4.85 us
  other arithmetic: 14.4 us -> 1.28 us
    psum x2 -> x0, waiting for transfers between devices: 357 us -> none  [spread(): return lax.psum(jnp.where(mine, shard, jnp.zeros_like(shard)), axis)]
    ppermute x0 -> x14, starting transfers between devices: none -> 24.5 us  [flip(): lax.ppermute(x, axis, [(i, i ^ d) for i in range(lax.axis_size(axis))])]
    pallas_call x0 -> x5, Pallas kernels: none -> 23.3 us  [the longest x1 8.74 us: per_device(): pl.pallas_call(functools.partial(product_kernel, sz), out_shape=jax.Shape...]
    ppermute x0 -> x14, waiting for transfers between devices: none -> 23.3 us  [flip(): lax.ppermute(x, axis, [(i, i ^ d) for i in range(lax.axis_size(axis))])]
    dot_general x4 -> x0, matrix products: 22.4 us -> none  [per_device(): jnp.dot(column_panel, row_panel, preferred_element_type=jnp.float32)]
    select_n x2 -> x0, other arithmetic: 13.7 us -> none  [spread(): return lax.psum(jnp.where(mine, shard, jnp.zeros_like(shard)), axis)]
    transpose x1 -> x0, local copies, waits for them, and re-layouts: 4.9 us -> none  [per_device(): grid.transpose(0, 2, 1, 3).reshape(LR * blocksz, col_count * blocksz)]
    scatter x1 -> x0, local copies, waits for them, and re-layouts: 4.89 us -> none  [per_device(): grid = jnp.zeros((LR, col_count, blocksz, blocksz), x_tiles.dtype).at[loc...]
  transfers between devices with their start and end apart: 2 -> 15, of which waited for: 2 -> 6; matrix products, arithmetic and copies ran while one was open for 2% -> 1% of each run, Pallas kernels for 0% -> 13%
where the time goes in v1:
time: 91.1 us; the launch traced here: 90.8 us
  starting transfers between devices  24.5 us (27%)
  Pallas kernels  23.3 us (26%)
  waiting for transfers between devices  23.3 us (26%)
  between operations  13.5 us (15%)
  local copies, waits for them, and re-layouts  4.85 us (5%)
  other arithmetic  1.28 us (1%)
    ppermute x14, starting transfers between devices, flip(): lax.ppermute(x, axis, [(i, i ^ d) for i in range(lax.axis_size(axis))])  24.5 us
    ppermute x14, waiting for transfers between devices, flip(): lax.ppermute(x, axis, [(i, i ^ d) for i in range(lax.axis_size(axis))])  23.3 us
    pallas_call x1, Pallas kernels, per_device(): pl.pallas_call(functools.partial(product_kernel, sz), out_shape=jax.Shape...  8.74 us
    pallas_call x1, Pallas kernels, per_device(): pl.pallas_call(functools.partial(row_meta_kernel, sz), out_shape=jax.Shap...  4.96 us
    unnamed x22, local copies, waits for them, and re-layouts  4.85 us
    pallas_call x1, Pallas kernels, per_device(): pl.pallas_call(functools.partial(column_meta_kernel, sz), out_shape=jax.S...  4.5 us
    pallas_call x1, Pallas kernels, per_device(): pl.pallas_call(functools.partial(pack_kernel, sz), out_shape=[jax.ShapeDt...  2.91 us
    pallas_call x1, Pallas kernels, per_device(): pl.pallas_call(functools.partial(hold_kernel, sz), out_shape=[jax.ShapeDt...  2.23 us
  transfers between devices with their start and end apart: 15, of which 6 were waited for; matrix products, arithmetic and copies ran while one was open for 1% of the time, Pallas kernels for 13%

profile of v1, /device:TPU:0, one launch (start us, length us, event | category | flops | bytes accessed | tf_op | source)
XLA Modules:
  0.0 90.8 jit_solution(11888969241613972457)
XLA Ops:
  6.5 0.0 all-gather.3.cloned.1.call-start
  6.5 2.9 %shard_map.37 = (bf16[528,128]{1,0:T(8,128)(2,1)}, bf16[528,128]{1,0:T(8,128)(2,1)}, bf16[528,128]{1,0:T(8,128)(2,1)}, bf16[528,128]{1,0:T(8,128)(2,1)}, bf16[27...) custom-call(s32[1,24]{1,0:T(1,128)} %pos_row_ref.1, ...), custom_call_target="tpu_custom_call" | custom-call | tf_op jit(solution)/shard_map/pallas_call | solution.py:239
  9.4 0.0 all-gather.3.cloned.1.call-update
  9.5 4.1 %collective-permute-start.3 = (bf16[272,128]{1,0:T(8,128)(2,1)}, bf16[272,128]{1,0:T(8,128)(2,1)S(1)}, u32[]{:S(2)}, u32[]{:S(2)}) collective-permute-start(bf16[272,128]{1,0:T(8,128)(2,1)} %get-tuple-element.21), channel_id=1, source_target_pairs={{0,16},{4,20},{8,24},{12,28},{16,0},{20,4},{24,8},{28,12},{1,17},{... | collective-permute-start | bytes 208904 | tf_op jit(solution)/shard_map/ppermute | solution.py:218
  13.6 1.3 %collective-permute-start.4 = (bf16[272,128]{1,0:T(8,128)(2,1)}, bf16[272,128]{1,0:T(8,128)(2,1)S(1)}, u32[]{:S(2)}, u32[]{:S(2)}) collective-permute-start(bf16[272,128]{1,0:T(8,128)(2,1)} %get-tuple-element.22), channel_id=1, source_target_pairs={{0,20},{4,16},{8,28},{12,24},{16,4},{20,0},{24,12},{28,8},{1,21},{... | collective-permute-start | bytes 208904 | tf_op jit(solution)/shard_map/ppermute | solution.py:218
  14.9 0.2 collective-permute-start
  15.1 1.8 %collective-permute-start.1 = (bf16[528,128]{1,0:T(8,128)(2,1)}, bf16[528,128]{1,0:T(8,128)(2,1)S(1)}, u32[]{:S(2)}, u32[]{:S(2)}) collective-permute-start(bf16[528,128]{1,0:T(8,128)(2,1)} %get-tuple-element.19), channel_id=1, source_target_pairs={{0,8},{4,12},{8,0},{12,4},{16,24},{20,28},{24,16},{28,20},{1,9},{5... | collective-permute-start | bytes 405512 | tf_op jit(solution)/shard_map/ppermute | solution.py:218
  16.9 1.4 %collective-permute-start.2 = (bf16[528,128]{1,0:T(8,128)(2,1)}, bf16[528,128]{1,0:T(8,128)(2,1)S(1)}, u32[]{:S(2)}, u32[]{:S(2)}) collective-permute-start(bf16[528,128]{1,0:T(8,128)(2,1)} %get-tuple-element.20), channel_id=1, source_target_pairs={{0,12},{4,8},{8,4},{12,0},{16,28},{20,24},{24,20},{28,16},{1,13},{... | collective-permute-start | bytes 405512 | tf_op jit(solution)/shard_map/ppermute | solution.py:218
  18.4 0.0 collective-permute-done.3.refs_4_
  18.4 4.5 %collective-permute-start.5 = (bf16[272,128]{1,0:T(8,128)(2,1)}, bf16[272,128]{1,0:T(8,128)(2,1)S(1)}, u32[]{:S(2)}, u32[]{:S(2)}) collective-permute-start(bf16[272,128]{1,0:T(8,128)(2,1)} %get-tuple-element.23), channel_id=1, source_target_pairs={{0,24},{4,28},{8,16},{12,20},{16,8},{20,12},{24,0},{28,4},{1,25},{... | collective-permute-start | bytes 208904 | tf_op jit(solution)/shard_map/ppermute | solution.py:218
  22.9 0.0 collective-permute-done.4.refs_5_
  22.9 2.3 %collective-permute-start.6 = (bf16[272,128]{1,0:T(8,128)(2,1)}, bf16[272,128]{1,0:T(8,128)(2,1)S(1)}, u32[]{:S(2)}, u32[]{:S(2)}) collective-permute-start(bf16[272,128]{1,0:T(8,128)(2,1)} %get-tuple-element.24), channel_id=1, source_target_pairs={{0,28},{4,24},{8,20},{12,16},{16,12},{20,8},{24,4},{28,0},{1,29},{... | collective-permute-start | bytes 208904 | tf_op jit(solution)/shard_map/ppermute | solution.py:218
  25.2 2.5 %collective-permute-done.5.refs_6_ = bf16[272,128]{1,0:T(8,128)(2,1)S(1)} collective-permute-done((bf16[272,128]{1,0:T(8,128)(2,1)}, bf16[272,128]{1,0:T(8,128)(2,1)S(1)}, u32[]{:S(2)}, u32[]{:S(2)}) %collective-permute-start.5) | collective-permute-done | bytes 69664 | tf_op jit(solution)/shard_map/ppermute | solution.py:218
  27.7 2.4 %collective-permute-done.6.refs_7_ = bf16[272,128]{1,0:T(8,128)(2,1)S(1)} collective-permute-done((bf16[272,128]{1,0:T(8,128)(2,1)}, bf16[272,128]{1,0:T(8,128)(2,1)S(1)}, u32[]{:S(2)}, u32[]{:S(2)}) %collective-permute-start.6) | collective-permute-done | bytes 69664 | tf_op jit(solution)/shard_map/ppermute | solution.py:218
  30.1 0.0 collective-permute-done.refs_1_
  30.1 0.0 collective-permute-done.1.refs_2_
  30.1 0.0 copy-start.5
  30.1 0.0 collective-permute-done.2.refs_3_
  30.1 0.0 copy-start.6
  30.1 0.0 copy-done.7
  30.2 0.5 copy-done.10
  30.7 0.1 copy-done.4
  30.8 0.1 copy-done.5
  30.8 0.0 copy-done.6
  30.9 2.2 %shard_map.39 = (bf16[1024,128]{1,0:T(8,128)(2,1)}, s32[8,24]{1,0:T(8,128)}) custom-call(s32[4]{0:T(128)} %panels_ref.7, bf16[528,128]{1,0:T(8,128)(2,1)} %get-tuple-element.17.refs_0_, bf16[528,128]{1,0:T(8,128)(2,1)} %copy-done.4, bf16[528,128]{1,0:T(8,128)(2,1)} %copy-done.5, bf16[528,128]{1,0:T(8,128)(2,1)} %copy-done.6, bf16[272,128]{1,0:T(8,128)(2,1)} %copy-done.7, ...), custom_call_target="tpu_custom_call" | custom-call | tf_op jit(solution)/shard_map/pallas_call | solution.py:250
  33.1 0.2 collective-permute-start.10
  33.3 3.5 %collective-permute-start.8 = (bf16[1024,128]{1,0:T(8,128)(2,1)}, bf16[1024,128]{1,0:T(8,128)(2,1)S(1)}, u32[]{:S(2)}, u32[]{:S(2)}) collective-permute-start(bf16[1024,128]{1,0:T(8,128)(2,1)} %get-tuple-element.26.refs_0_), channel_id=1, source_target_pairs={{0,8},{4,12},{8,0},{12,4},{16,24},{20,28},{24,16},{28,20},{1,9},{5... | collective-permute-start | bytes 786440 | tf_op jit(solution)/shard_map/ppermute | solution.py:218
  36.8 10.0 %collective-permute-done.10.refs_4_ = bf16[1024,128]{1,0:T(8,128)(2,1)S(1)} collective-permute-done((bf16[1024,128]{1,0:T(8,128)(2,1)}, bf16[1024,128]{1,0:T(8,128)(2,1)S(1)}, u32[]{:S(2)}, u32[]{:S(2)}) %collective-permute-start.10) | collective-permute-done | bytes 262176 | tf_op jit(solution)/shard_map/ppermute | solution.py:218
  46.8 0.0 collective-permute-start.12
  46.8 0.7 collective-permute-start.7
  47.5 1.3 %collective-permute-start.11 = (bf16[1024,128]{1,0:T(8,128)(2,1)S(1)}, bf16[1024,128]{1,0:T(8,128)(2,1)S(1)}, u32[]{:S(2)}, u32[]{:S(2)}) collective-permute-start(bf16[1024,128]{1,0:T(8,128)(2,1)S(1)} %collective-permute-done.10.refs_4_), channel_id=1, source_target_pairs={{0,4},{4,0},{8,12},{12,8},{16,20},{20,16},{24,28},{28,24},{1,5},{5... | collective-permute-start | bytes 786440 | tf_op jit(solution)/shard_map/ppermute | solution.py:218
  48.8 0.0 collective-permute-done.8.refs_2_
  48.8 0.7 collective-permute-start.9
  49.6 3.9 %collective-permute-done.12.refs_6_ = bf16[1024,128]{1,0:T(8,128)(2,1)S(1)} collective-permute-done((bf16[1024,128]{1,0:T(8,128)(2,1)S(1)}, bf16[1024,128]{1,0:T(8,128)(2,1)S(1)}, u32[]{:S(2)}, u32[]{:S(2)}) %collective-permute-start.12) | collective-permute-done | bytes 262176 | tf_op jit(solution)/shard_map/ppermute | solution.py:218
  53.4 2.3 %collective-permute-start.13 = (bf16[1024,128]{1,0:T(8,128)(2,1)S(1)}, bf16[1024,128]{1,0:T(8,128)(2,1)S(1)}, u32[]{:S(2)}, u32[]{:S(2)}) collective-permute-start(bf16[1024,128]{1,0:T(8,128)(2,1)S(1)} %collective-permute-done.12.refs_6_), channel_id=1, source_target_pairs={{0,4},{4,0},{8,12},{12,8},{16,20},{20,16},{24,28},{28,24},{1,5},{5... | collective-permute-start | bytes 786440 | tf_op jit(solution)/shard_map/ppermute | solution.py:218
  55.7 4.5 %shard_map.40.b_list = s32[64]{0:T(128)} custom-call(s32[8,24]{1,0:T(8,128)} %get-tuple-element.25.notes_ref, s32[4]{0:T(128)} %panels_ref.7), custom_call_target="tpu_custom_call" | custom-call | tf_op jit(solution)/shard_map/pallas_call | solution.py:261
  60.2 0.0 all-gather.3.cloned.1.call-done
  60.2 1.3 %slice_convert_fusion = s32[4,1,24]{2,1,0:T(1,128)} fusion(bf16[4,3088,128]{2,1,0:T(8,128)(2,1)} %bitcast.2), kind=kLoop, calls=%fused_computation | loop fusion | flops 96 | bytes 576 | tf_op jit(solution)/shard_map/convert_element_type | solution.py:272
  61.5 5.0 %shard_map.38.a_list = s32[136]{0:T(256)} custom-call(s32[4,24]{1,0:T(4,128)} %bitcast.4, s32[4]{0:T(128)} %panels_ref.7), custom_call_target="tpu_custom_call" | custom-call | tf_op jit(solution)/shard_map/pallas_call | solution.py:267
  66.5 0.0 collective-permute-done.7.refs_1_
  66.5 0.0 collective-permute-done.11.refs_5_
  66.5 1.0 %collective-permute-done.9.refs_3_ = bf16[1024,128]{1,0:T(8,128)(2,1)S(1)} collective-permute-done((bf16[1024,128]{1,0:T(8,128)(2,1)S(1)}, bf16[1024,128]{1,0:T(8,128)(2,1)S(1)}, u32[]{:S(2)}, u32[]{:S(2)}) %collective-permute-start.9) | collective-permute-done | bytes 262176 | tf_op jit(solution)/shard_map/ppermute | solution.py:218
  67.5 3.5 %collective-permute-done.13.refs_7_ = bf16[1024,128]{1,0:T(8,128)(2,1)S(1)} collective-permute-done((bf16[1024,128]{1,0:T(8,128)(2,1)S(1)}, bf16[1024,128]{1,0:T(8,128)(2,1)S(1)}, u32[]{:S(2)}, u32[]{:S(2)}) %collective-permute-start.13) | collective-permute-done | bytes 262176 | tf_op jit(solution)/shard_map/ppermute | solution.py:218
  71.0 1.9 %copy-done = bf16[12352,128]{1,0:T(8,128)(2,1)S(1)} copy-done((bf16[12352,128]{1,0:T(8,128)(2,1)S(1)}, bf16[12352,128]{1,0:T(8,128)(2,1)}, u32[]{:S(2)}) %copy-start) | copy-done | bytes 3162136
  72.9 0.9 %copy-done.1 = bf16[1024,128]{1,0:T(8,128)(2,1)S(1)} copy-done((bf16[1024,128]{1,0:T(8,128)(2,1)S(1)}, bf16[1024,128]{1,0:T(8,128)(2,1)}, u32[]{:S(2)}) %copy-start.1) | copy-done | bytes 262168
  73.9 0.7 copy-done.2
  74.5 0.6 copy-done.3
  75.2 8.7 %shard_map.41 = f32[1024,2048]{1,0:T(8,128)} custom-call(s32[136]{0:T(256)S(1)} %copy-done.2, s32[64]{0:T(128)S(1)} %copy-done.3, bf16[4,3088,128]{2,1,0:T(8,128)(2,1)S(1)} %bitcast.3, bf16[1024,128]{1,0:T(8,128)(2,1)S(1)} %copy-done.1, bf16[1024,128]{1,0:T(8,128)(2,1)S(1)} %collective-permute-done.7.refs_1_, ...), custom_call_target="tpu_custom_call" | custom-call | flops 2000000000 | bytes 12582912 | tf_op jit(solution)/shard_map/pallas_call | solution.py:275
  (11 shorter events, 0.0 us)
Async XLA Ops:
  6.5 53.7 %all-gather.3.cloned.1.call-start = ((), (), s32[]{:S(2)}) async-start(), calls=%async_computation | async-start | bytes 3952640 | tf_op jit(solution)/shard_map/all_gather | solution.py:248
  9.5 8.9 %collective-permute-start.3 = (bf16[272,128]{1,0:T(8,128)(2,1)}, bf16[272,128]{1,0:T(8,128)(2,1)S(1)}, u32[]{:S(2)}, u32[]{:S(2)}) collective-permute-start(bf16[272,128]{1,0:T(8,128)(2,1)} %get-tuple-element.21), channel_id=1, source_target_pairs={{0,16},{4,20},{8,24},{12,28},{16,0},{20,4},{24,8},{28,12},{1,17},{... | collective-permute-start | bytes 208904 | tf_op jit(solution)/shard_map/ppermute | solution.py:218
  13.6 9.3 %collective-permute-start.4 = (bf16[272,128]{1,0:T(8,128)(2,1)}, bf16[272,128]{1,0:T(8,128)(2,1)S(1)}, u32[]{:S(2)}, u32[]{:S(2)}) collective-permute-start(bf16[272,128]{1,0:T(8,128)(2,1)} %get-tuple-element.22), channel_id=1, source_target_pairs={{0,20},{4,16},{8,28},{12,24},{16,4},{20,0},{24,12},{28,8},{1,21},{... | collective-permute-start | bytes 208904 | tf_op jit(solution)/shard_map/ppermute | solution.py:218
  14.9 15.2 %collective-permute-start = (bf16[528,128]{1,0:T(8,128)(2,1)}, bf16[528,128]{1,0:T(8,128)(2,1)S(1)}, u32[]{:S(2)}, u32[]{:S(2)}) collective-permute-start(bf16[528,128]{1,0:T(8,128)(2,1)} %get-tuple-element.18), channel_id=1, source_target_pairs={{0,4},{4,0},{8,12},{12,8},{16,20},{20,16},{24,28},{28,24},{1,5},{5... | collective-permute-start | bytes 405512 | tf_op jit(solution)/shard_map/ppermute | solution.py:218
  15.1 15.0 %collective-permute-start.1 = (bf16[528,128]{1,0:T(8,128)(2,1)}, bf16[528,128]{1,0:T(8,128)(2,1)S(1)}, u32[]{:S(2)}, u32[]{:S(2)}) collective-permute-start(bf16[528,128]{1,0:T(8,128)(2,1)} %get-tuple-element.19), channel_id=1, source_target_pairs={{0,8},{4,12},{8,0},{12,4},{16,24},{20,28},{24,16},{28,20},{1,9},{5... | collective-permute-start | bytes 405512 | tf_op jit(solution)/shard_map/ppermute | solution.py:218
  16.9 13.2 %collective-permute-start.2 = (bf16[528,128]{1,0:T(8,128)(2,1)}, bf16[528,128]{1,0:T(8,128)(2,1)S(1)}, u32[]{:S(2)}, u32[]{:S(2)}) collective-permute-start(bf16[528,128]{1,0:T(8,128)(2,1)} %get-tuple-element.20), channel_id=1, source_target_pairs={{0,12},{4,8},{8,4},{12,0},{16,28},{20,24},{24,20},{28,16},{1,13},{... | collective-permute-start | bytes 405512 | tf_op jit(solution)/shard_map/ppermute | solution.py:218
  18.4 11.8 %copy-start.7 = (bf16[272,128]{1,0:T(8,128)(2,1)}, bf16[272,128]{1,0:T(8,128)(2,1)S(1)}, u32[]{:S(2)}) copy-start(bf16[272,128]{1,0:T(8,128)(2,1)S(1)} %collective-permute-done.3.refs_4_) | copy-start | bytes 208900
  18.4 9.3 %collective-permute-start.5 = (bf16[272,128]{1,0:T(8,128)(2,1)}, bf16[272,128]{1,0:T(8,128)(2,1)S(1)}, u32[]{:S(2)}, u32[]{:S(2)}) collective-permute-start(bf16[272,128]{1,0:T(8,128)(2,1)} %get-tuple-element.23), channel_id=1, source_target_pairs={{0,24},{4,28},{8,16},{12,20},{16,8},{20,12},{24,0},{28,4},{1,25},{... | collective-permute-start | bytes 208904 | tf_op jit(solution)/shard_map/ppermute | solution.py:218
  22.9 7.3 %copy-start.8 = (bf16[272,128]{1,0:T(8,128)(2,1)}, bf16[272,128]{1,0:T(8,128)(2,1)S(1)}, u32[]{:S(2)}) copy-start(bf16[272,128]{1,0:T(8,128)(2,1)S(1)} %collective-permute-done.4.refs_5_) | copy-start | bytes 208900
  22.9 7.2 %collective-permute-start.6 = (bf16[272,128]{1,0:T(8,128)(2,1)}, bf16[272,128]{1,0:T(8,128)(2,1)S(1)}, u32[]{:S(2)}, u32[]{:S(2)}) collective-permute-start(bf16[272,128]{1,0:T(8,128)(2,1)} %get-tuple-element.24), channel_id=1, source_target_pairs={{0,28},{4,24},{8,20},{12,16},{16,12},{20,8},{24,4},{28,0},{1,29},{... | collective-permute-start | bytes 208904 | tf_op jit(solution)/shard_map/ppermute | solution.py:218
  27.7 2.5 %copy-start.9 = (bf16[272,128]{1,0:T(8,128)(2,1)}, bf16[272,128]{1,0:T(8,128)(2,1)S(1)}, u32[]{:S(2)}) copy-start(bf16[272,128]{1,0:T(8,128)(2,1)S(1)} %collective-permute-done.5.refs_6_) | copy-start | bytes 208900
  30.1 0.6 copy-start.10
  30.1 0.7 copy-start.4
  30.1 0.7 copy-start.5
  30.1 0.7 copy-start.6
  33.1 13.7 %collective-permute-start.10 = (bf16[1024,128]{1,0:T(8,128)(2,1)}, bf16[1024,128]{1,0:T(8,128)(2,1)S(1)}, u32[]{:S(2)}, u32[]{:S(2)}) collective-permute-start(bf16[1024,128]{1,0:T(8,128)(2,1)} %get-tuple-element.26.refs_0_), channel_id=1, source_target_pairs={{0,16},{4,20},{8,24},{12,28},{16,0},{20,4},{24,8},{28,12},{1,17},{... | collective-permute-start | bytes 786440 | tf_op jit(solution)/shard_map/ppermute | solution.py:218
  33.3 15.6 %collective-permute-start.8 = (bf16[1024,128]{1,0:T(8,128)(2,1)}, bf16[1024,128]{1,0:T(8,128)(2,1)S(1)}, u32[]{:S(2)}, u32[]{:S(2)}) collective-permute-start(bf16[1024,128]{1,0:T(8,128)(2,1)} %get-tuple-element.26.refs_0_), channel_id=1, source_target_pairs={{0,8},{4,12},{8,0},{12,4},{16,24},{20,28},{24,16},{28,20},{1,9},{5... | collective-permute-start | bytes 786440 | tf_op jit(solution)/shard_map/ppermute | solution.py:218
  46.8 6.6 %collective-permute-start.12 = (bf16[1024,128]{1,0:T(8,128)(2,1)S(1)}, bf16[1024,128]{1,0:T(8,128)(2,1)S(1)}, u32[]{:S(2)}, u32[]{:S(2)}) collective-permute-start(bf16[1024,128]{1,0:T(8,128)(2,1)S(1)} %collective-permute-done.10.refs_4_), channel_id=1, source_target_pairs={{0,8},{4,12},{8,0},{12,4},{16,24},{20,28},{24,16},{28,20},{1,9},{5... | collective-permute-start | bytes 786440 | tf_op jit(solution)/shard_map/ppermute | solution.py:218
  46.8 19.7 %collective-permute-start.7 = (bf16[1024,128]{1,0:T(8,128)(2,1)}, bf16[1024,128]{1,0:T(8,128)(2,1)S(1)}, u32[]{:S(2)}, u32[]{:S(2)}) collective-permute-start(bf16[1024,128]{1,0:T(8,128)(2,1)} %get-tuple-element.26.refs_0_), channel_id=1, source_target_pairs={{0,4},{4,0},{8,12},{12,8},{16,20},{20,16},{24,28},{28,24},{1,5},{5... | collective-permute-start | bytes 786440 | tf_op jit(solution)/shard_map/ppermute | solution.py:218
  47.5 19.0 %collective-permute-start.11 = (bf16[1024,128]{1,0:T(8,128)(2,1)S(1)}, bf16[1024,128]{1,0:T(8,128)(2,1)S(1)}, u32[]{:S(2)}, u32[]{:S(2)}) collective-permute-start(bf16[1024,128]{1,0:T(8,128)(2,1)S(1)} %collective-permute-done.10.refs_4_), channel_id=1, source_target_pairs={{0,4},{4,0},{8,12},{12,8},{16,20},{20,16},{24,28},{28,24},{1,5},{5... | collective-permute-start | bytes 786440 | tf_op jit(solution)/shard_map/ppermute | solution.py:218
  48.8 18.7 %collective-permute-start.9 = (bf16[1024,128]{1,0:T(8,128)(2,1)S(1)}, bf16[1024,128]{1,0:T(8,128)(2,1)S(1)}, u32[]{:S(2)}, u32[]{:S(2)}) collective-permute-start(bf16[1024,128]{1,0:T(8,128)(2,1)S(1)} %collective-permute-done.8.refs_2_), channel_id=1, source_target_pairs={{0,4},{4,0},{8,12},{12,8},{16,20},{20,16},{24,28},{28,24},{1,5},{5... | collective-permute-start | bytes 786440 | tf_op jit(solution)/shard_map/ppermute | solution.py:218
  53.4 17.6 %collective-permute-start.13 = (bf16[1024,128]{1,0:T(8,128)(2,1)S(1)}, bf16[1024,128]{1,0:T(8,128)(2,1)S(1)}, u32[]{:S(2)}, u32[]{:S(2)}) collective-permute-start(bf16[1024,128]{1,0:T(8,128)(2,1)S(1)} %collective-permute-done.12.refs_6_), channel_id=1, source_target_pairs={{0,4},{4,0},{8,12},{12,8},{16,20},{20,16},{24,28},{28,24},{1,5},{5... | collective-permute-start | bytes 786440 | tf_op jit(solution)/shard_map/ppermute | solution.py:218
  71.0 1.9 %copy-start = (bf16[12352,128]{1,0:T(8,128)(2,1)S(1)}, bf16[12352,128]{1,0:T(8,128)(2,1)}, u32[]{:S(2)}) copy-start(bf16[12352,128]{1,0:T(8,128)(2,1)} %all-gather.3.cloned.1.call-done) | copy-start | bytes 9486340
  72.9 0.9 %copy-start.1 = (bf16[1024,128]{1,0:T(8,128)(2,1)S(1)}, bf16[1024,128]{1,0:T(8,128)(2,1)}, u32[]{:S(2)}) copy-start(bf16[1024,128]{1,0:T(8,128)(2,1)} %get-tuple-element.26.refs_0_) | copy-start | bytes 786436
  73.9 0.7 copy-start.2
  74.5 0.6 copy-start.3
Sparse Core Ops, SparseCore 0:
  9.6 31.3 all-gather.2

commit v2 on v1

v2 whole, which is shorter than its diff:
```python
import functools

import jax
import jax.numpy as jnp
from jax import lax
from jax.experimental import pallas as pl
from jax.experimental.pallas import tpu as pltpu
from jax.sharding import PartitionSpec as P

LR = 8
PW = 4
SECTIONS = 4
QD = 10
QS = 2
NOTE = 16
AT_ONCE = 8


class Sizes:
    def __init__(self, rows, cols, slots, bs):
        self.rows, self.cols, self.slots, self.bs = rows, cols, slots, bs
        self.lc = LR * rows // cols
        self.panels = rows * LR // PW
        panel_most = (self.lc // PW) * QS + (QD - QS)
        self.share = -(-panel_most // rows)
        self.near = -(-max(0, slots - rows * self.share) // self.share)
        self.held = SECTIONS * self.share
        self.depth = SECTIONS * PW
        self.late = [d * self.held + h for d in range(rows) if d & 1 and d & (rows // 2) for h in range(self.held)]

    def given(self, d):
        return self.share * (2 if d < self.near else 1)


def list_sections(sz, panels_ref, section_ref):
    for p in range(sz.panels):
        section_ref[p] = -1
    for j in range(SECTIONS):
        section_ref[panels_ref[j]] = j


def owned_by(panels_ref, row):
    count, first, last = jnp.int32(0), jnp.int32(-1), jnp.int32(0)
    for j in reversed(range(SECTIONS)):
        mine = lax.div(panels_ref[j], LR // PW) == row
        last = jnp.where(mine & (count == 0), j, last)
        first = jnp.where(mine, j, first)
        count = count + mine.astype(jnp.int32)
    return count, first, last


def deal(sz, count, picked, e, i):
    i = jnp.where(picked, i + 1, i)
    full = i == jnp.where((count == 2) & (e < sz.near), 2 * sz.share, sz.share)
    return jnp.where(full, e + 1, e), jnp.where(full, 0, i)


def pack_kernel(sz, pos_ref, panels_ref, pos_row_ref, x_ref, *refs):
    outs, (all_ref, section_ref, plan_ref, src_ref) = refs[: sz.rows], refs[sz.rows :]
    row = lax.axis_index("row")
    count, _, _ = owned_by(panels_ref, row)
    bs, most = sz.bs, 2 * sz.share
    for e in range(sz.rows * most):
        src_ref[e] = 0
    list_sections(sz, panels_ref, section_ref)
    for d in range(sz.rows):
        for i, value in enumerate(owned_by(panels_ref, row ^ d)):
            plan_ref[3 * d + i] = value

    def one(s, state):
        e, i = state
        picked = section_ref[row * (LR // PW) + lax.div(pos_ref[0, s], sz.lc * PW)] >= 0

        @pl.when(picked)
        def _():
            src_ref[e * most + i] = s

        return deal(sz, count, picked, e, i)

    lax.fori_loop(0, sz.slots, one, (jnp.int32(0), jnp.int32(0)))
    note = jnp.broadcast_to(pos_row_ref[...].astype(jnp.float32), (NOTE, sz.slots)).astype(x_ref.dtype)
    for e in range(sz.rows):
        for i in range(sz.given(e)):
            outs[e][i * bs : (i + 1) * bs] = x_ref[src_ref[e * most + i]]
        outs[e][sz.given(e) * bs :, : sz.slots] = note
    for s in range(sz.slots):
        all_ref[s * bs : (s + 1) * bs] = x_ref[s]
    all_ref[sz.slots * bs :, : sz.slots] = note


def hold_kernel(sz, plan_ref, *refs):
    came, hold_ref, notes_ref = refs[: sz.rows], refs[sz.rows], refs[sz.rows + 1]
    n = sz.share * sz.bs

    for d in range(sz.rows):
        note = came[d][sz.given(d) * sz.bs :].astype(jnp.float32)[:1, : sz.slots]
        notes_ref[d : d + 1, :] = note.astype(jnp.int32)
    for d in range(sz.rows):
        count, first, last = (plan_ref[3 * d + i] for i in range(3))

        @pl.when(count > 0)
        def _():
            hold_ref[pl.ds(pl.multiple_of(first * n, n), n)] = came[d][:n]

        if d < sz.near:

            @pl.when(count == 2)
            def _():
                hold_ref[pl.ds(pl.multiple_of(last * n, n), n)] = came[d][n : 2 * n]


def column_meta_kernel(sz, notes_ref, section_ref, plan_ref, b_list, b_dense):
    row = lax.axis_index("row")
    b_dense[...] = jnp.zeros_like(b_dense)

    for i in range(sz.rows * sz.held):
        b_list[i] = -1

    def one_row(d, _):
        count, first, last = (plan_ref[3 * d + i] for i in range(3))
        owner = row ^ d

        def one(s, state):
            e, i = state
            pos = notes_ref[d, s]
            local_row, local_col = lax.div(pos, sz.lc), lax.rem(pos, sz.lc)
            section = section_ref[owner * (LR // PW) + lax.div(local_row, PW)]
            picked = section >= 0

            @pl.when(picked)
            def _():
                at = jnp.where(i < sz.share, first * sz.share + i, last * sz.share + i - sz.share)
                b_list[(d ^ e) * sz.held + at] = (section * PW + lax.rem(local_row, PW)) * sz.lc + local_col

            return deal(sz, count, picked, e, i)

        @pl.when(count > 0)
        def _():
            lax.fori_loop(0, sz.slots, one, (jnp.int32(0), jnp.int32(0)))

        return 0

    lax.fori_loop(0, sz.rows, one_row, 0)


def row_meta_kernel(sz, notes_ref, section_ref, b_list, *refs):
    a_refs, (a_list, late_list, a_sorted, by_k, latest) = refs[: sz.cols], refs[sz.cols :]
    col = lax.axis_index("col")
    bs, depth = sz.bs, sz.depth
    for i in range(LR):
        a_list[i * (depth + 1)] = 0
    for k in range(depth):
        by_k[k * (LR + 1)] = 0

    for e in range(sz.cols):

        def one(s, _):
            pos = notes_ref[e, s]
            local_row, local_col = lax.div(pos, sz.lc), lax.rem(pos, sz.lc)
            section = section_ref[(e ^ col) * (sz.lc // PW) + lax.div(local_col, PW)]

            @pl.when(section >= 0)
            def _():
                k = section * PW + lax.rem(local_col, PW)
                base = local_row * (depth + 1)
                n = a_list[base]
                a_list[base + 1 + n] = k
                a_list[base] = n + 1
                place = local_row * depth + n
                base = k * (LR + 1)
                n = by_k[base]
                by_k[base + 1 + n] = place
                by_k[base] = n + 1
                a_sorted[place] = a_refs[e][pl.ds(pl.multiple_of(s * bs, bs), bs), :]

            return 0

        lax.fori_loop(0, sz.slots, one, 0)

    total = jnp.int32(0)
    for h, at_place in enumerate(sz.late):
        at = b_list[at_place]
        there = at >= 0
        at = jnp.maximum(at, 0)
        base, c = lax.div(at, sz.lc) * (LR + 1), lax.rem(at, sz.lc)
        n = jnp.where(there, by_k[base], 0)

        def pair(t, _):
            place = by_k[base + 1 + t]
            tile = lax.div(place, depth) * sz.lc + c
            late_list[2 + 2 * (total + t)] = h * (LR * depth) + place
            late_list[3 + 2 * (total + t)] = tile
            latest[tile] = total + t
            return 0

        lax.fori_loop(0, n, pair, 0)
        total = total + n

    def mark(t, tiles):
        tile = late_list[3 + 2 * t]
        last = (latest[tile] == t).astype(jnp.int32)
        late_list[3 + 2 * t] = 2 * tile + last
        return tiles + last

    late_list[0] = total
    late_list[1] = lax.fori_loop(0, total, mark, jnp.int32(0))


def tile(sz, i, c):
    return pl.ds(pl.multiple_of(i * sz.bs, sz.bs), sz.bs), pl.ds(pl.multiple_of(c * sz.bs, sz.bs), sz.bs)


def product_kernel(sz, starts, a_list, b_list, b_clear, a_sorted, *refs):
    b_refs, (total, out_ref, b_dense, sem) = refs[: len(starts)], refs[len(starts) :]
    bs, depth = sz.bs, sz.depth
    for start, b_ref in zip(starts, b_refs):
        for h in range(b_ref.shape[0] // bs):
            at = b_list[start + h]

            @pl.when(at >= 0)
            def _():
                k, c = lax.div(at, sz.lc), lax.rem(at, sz.lc)
                b_dense[k, :, pl.ds(pl.multiple_of(c * bs, bs), bs)] = b_ref[h * bs : (h + 1) * bs]

    width = total.shape[1]
    chunk = min(width, 512)

    def to_out(i):
        here = pl.ds(pl.multiple_of(i * bs, bs), bs)
        return pltpu.make_async_copy(total.at[here], out_ref.at[here], sem)

    def one_row(i, _):
        base = i * (depth + 1)
        n = a_list[base]
        here = pl.ds(pl.multiple_of(i * bs, bs), bs)

        def group(start, size, first):
            ks, blocks = [], []
            for t in range(size):
                at = jnp.minimum(start + t, depth - 1)
                there = start + t < n
                block = a_sorted[i * depth + at]
                blocks.append(jnp.where(there, block, jnp.zeros_like(block)))
                ks.append(jnp.where(there, a_list[base + 1 + at], 0))
            lhs = jnp.concatenate(blocks, axis=1)
            for c in range(0, width, chunk):
                rhs = jnp.concatenate([b_dense[k, :, c : c + chunk] for k in ks], axis=0)
                part = jnp.dot(lhs, rhs, preferred_element_type=jnp.float32)
                if first:
                    total[here, c : c + chunk] = part
                else:
                    total[here, c : c + chunk] += part

        @pl.when(n <= 2)
        def _():
            group(0, 2, True)

        @pl.when(n > 2)
        def _():
            group(0, 4, True)

        def more(g, _):
            group(4 + 2 * g, 2, False)
            return 0

        lax.fori_loop(0, lax.div(jnp.maximum(n - 3, 0), 2), more, 0)
        to_out(i).start()
        return 0

    lax.fori_loop(0, LR, one_row, 0)

    def done(i, _):
        to_out(i).wait()
        return 0

    lax.fori_loop(0, LR, done, 0)


def last_kernel(sz, late_list, total_in, out_in, a_sorted, *refs):
    b_refs, (total, out_ref, right, parts, sem) = refs[:-5], refs[-5:]
    bs, every = sz.bs, LR * sz.depth
    count = late_list[0]
    at = 0
    for b_ref in b_refs:
        for h in range(b_ref.shape[0] // bs):
            right[at] = b_ref[h * bs : (h + 1) * bs]
            at += 1

    def to_out(at):
        return pltpu.make_async_copy(total.at[at], out_ref.at[at], sem)

    def group(g, _):
        for u in range(AT_ONCE):
            code = late_list[2 + 2 * jnp.minimum(g * AT_ONCE + u, count - 1)]
            parts[u] = jnp.dot(
                a_sorted[lax.rem(code, every)], right[lax.div(code, every)], preferred_element_type=jnp.float32
            )
        for u in range(AT_ONCE):
            t = g * AT_ONCE + u

            @pl.when(t < count)
            def _():
                code = late_list[3 + 2 * t]
                at = tile(sz, lax.div(code, 2 * sz.lc), lax.rem(lax.div(code, 2), sz.lc))
                total[at] += parts[u]

                @pl.when(lax.rem(code, 2) == 1)
                def _():
                    to_out(at).start()

        return 0

    lax.fori_loop(0, lax.div(count + AT_ONCE - 1, AT_ONCE), group, 0)

    def done(t, _):
        to_out((slice(0, bs), slice(0, bs))).wait()
        return 0

    lax.fori_loop(0, late_list[1], done, 0)


def flip(x, axis, d):
    return lax.ppermute(x, axis, [(i, i ^ d) for i in range(lax.axis_size(axis))])


def gather_by_flips(x, axis):
    n = lax.axis_size(axis)
    got, bit = {0: x}, n // 2
    while bit:
        for d in list(got):
            got[d | bit] = flip(got[d], axis, bit)
        bit //= 2
    return [got[d] for d in range(n)]


def per_device(x_tiles, tile_pos, panel_ids):
    rows, cols = lax.axis_size("row"), lax.axis_size("col")
    slots, bs, _ = x_tiles.shape
    dtype = x_tiles.dtype
    sz = Sizes(rows, cols, slots, bs)
    smem = pl.BlockSpec(memory_space=pltpu.SMEM)
    vmem = pl.BlockSpec(memory_space=pltpu.VMEM)

    *parts, mine, sections, plan = pl.pallas_call(
        functools.partial(pack_kernel, sz),
        out_shape=[pltpu.VMEM((sz.given(d) * bs + NOTE, bs), dtype) for d in range(rows)]
        + [
            pltpu.VMEM((slots * bs + NOTE, bs), dtype),
            pltpu.SMEM((sz.panels,), jnp.int32),
            pltpu.SMEM((3 * rows,), jnp.int32),
        ],
        in_specs=[smem, smem, vmem, vmem],
        out_specs=[vmem] * (rows + 1) + [smem, smem],
        scratch_shapes=[pltpu.SMEM((rows * 2 * sz.share,), jnp.int32)],
    )(tile_pos, panel_ids, tile_pos, x_tiles)

    in_vmem = functools.partial(pltpu.with_memory_space_constraint, memory_space=pltpu.VMEM)
    in_smem = functools.partial(pltpu.with_memory_space_constraint, memory_space=pltpu.SMEM)
    sections, plan = in_smem(sections), in_smem(plan)
    a_got, a_bit = {0: mine}, cols // 2
    a_got[a_bit] = flip(mine, "col", a_bit)
    came = [parts[0]] + [flip(parts[d], "row", d) for d in range(1, rows)]
    hold, column_notes = pl.pallas_call(
        functools.partial(hold_kernel, sz),
        out_shape=[
            pltpu.VMEM((sz.held * bs, bs), dtype),
            jax.ShapeDtypeStruct((rows, slots), jnp.int32),
        ],
        in_specs=[smem] + [vmem] * rows,
        out_specs=[vmem, vmem],
    )(plan, *map(in_vmem, came))
    width = sz.lc * bs
    params = pltpu.CompilerParams(vmem_limit_bytes=32 * 2**20)
    b_list, b_clear = pl.pallas_call(
        functools.partial(column_meta_kernel, sz),
        out_shape=[
            pltpu.SMEM((rows * sz.held,), jnp.int32),
            pltpu.VMEM((sz.depth, bs, width), dtype),
        ],
        in_specs=[smem, smem, smem],
        out_specs=[smem, vmem],
        compiler_params=params,
    )(column_notes, sections, plan)

    bits = [1 << b for b in reversed(range(rows.bit_length() - 1))]
    a_got, hold_too = lax.optimization_barrier((a_got, hold))
    got = {0: [hold], **{bit: [flip(hold_too if bit < bits[0] else hold, "row", bit)] for bit in bits}}
    while a_bit:
        for d in list(a_got):
            if d | a_bit not in a_got:
                a_got[d | a_bit] = flip(a_got[d], "col", a_bit)
        a_bit //= 2
    a_parts = [a_got[d] for d in range(cols)]
    row_notes = jnp.stack([a[-1, :slots] for a in a_parts]).astype(jnp.int32)
    a_list, late_list, a_sorted = pl.pallas_call(
        functools.partial(row_meta_kernel, sz),
        out_shape=[
            pltpu.SMEM((LR * (sz.depth + 1),), jnp.int32),
            pltpu.SMEM((2 + 2 * len(sz.late) * LR,), jnp.int32),
            pltpu.VMEM((LR * sz.depth, bs, bs), dtype),
        ],
        in_specs=[smem] * 3 + [vmem] * cols,
        out_specs=[smem, smem, vmem],
        scratch_shapes=[
            pltpu.SMEM((sz.depth * (LR + 1),), jnp.int32),
            pltpu.SMEM((LR * sz.lc,), jnp.int32),
        ],
        compiler_params=params,
    )(row_notes, sections, in_smem(b_list), *map(in_vmem, a_parts))
    got[2], a_list, a_sorted = lax.optimization_barrier((got[2], a_list, a_sorted))
    if 3 not in got:
        got[3] = [flip(got[2][0], "row", 1)]
    (top, second), half = bits[:2], sz.held * bs // 2
    got[top], got[2], got[1], a_list, a_sorted = lax.optimization_barrier(
        (got[top], got[2], got[1], a_list, a_sorted)
    )
    first, rest = got[top][0][:half], got[top][0][half:]
    first, rest = flip(first, "row", second), flip(rest, "row", second)
    rest, got[3] = lax.optimization_barrier((rest, got[3]))
    got[top | second] = [first, rest]
    got[top | second | 1] = [flip(p, "row", 1) for p in got[top | second]]
    got[top | 1] = [flip(got[top][0][:half], "row", 1), flip(got[1][0][half:], "row", top)]
    for bit in bits[1:]:
        for d in list(got):
            if d | bit not in got:
                got[d | bit] = [flip(p, "row", bit) for p in got[d]]

    early, late = [], []
    for d in range(rows):
        for i, piece in enumerate(got[d]):
            if d * sz.held in sz.late:
                late.append(in_vmem(piece))
            else:
                early.append((d * sz.held + i * half // bs, in_vmem(piece)))

    total, out = pl.pallas_call(
        functools.partial(product_kernel, sz, [start for start, _ in early]),
        out_shape=[
            pltpu.VMEM((LR * bs, width), jnp.float32),
            jax.ShapeDtypeStruct((LR * bs, width), jnp.float32),
            pltpu.VMEM((sz.depth, bs, width), dtype),
        ],
        in_specs=[smem, smem] + [vmem] * (2 + len(early)),
        out_specs=[vmem, pl.BlockSpec(memory_space=pl.ANY), vmem],
        input_output_aliases={2: 2},
        scratch_shapes=[pltpu.SemaphoreType.DMA],
        compiler_params=params,
        cost_estimate=pl.CostEstimate(flops=2 * 10**9, bytes_accessed=12 * 2**20, transcendentals=0),
    )(in_smem(a_list), in_smem(b_list), in_vmem(b_clear), in_vmem(a_sorted), *(b for _, b in early))[:2]
    return pl.pallas_call(
        functools.partial(last_kernel, sz),
        out_shape=[
            pltpu.VMEM((LR * bs, width), jnp.float32),
            jax.ShapeDtypeStruct((LR * bs, width), jnp.float32),
        ],
        in_specs=[smem, vmem, pl.BlockSpec(memory_space=pl.ANY), vmem] + [vmem] * len(late),
        out_specs=[vmem, pl.BlockSpec(memory_space=pl.ANY)],
        input_output_aliases={1: 0, 2: 1},
        scratch_shapes=[
            pltpu.VMEM((len(sz.late), bs, bs), dtype),
            pltpu.VMEM((AT_ONCE, bs, bs), jnp.float32),
            pltpu.SemaphoreType.DMA,
        ],
        compiler_params=params,
    )(in_smem(late_list), in_vmem(total), out, in_vmem(a_sorted), *late)[1]


def solution(mesh):
    in_specs = (P("row", "col", None), P("row", "col"), P())
    out_specs = P("row", "col")
    return jax.shard_map(
        per_device, mesh=mesh, in_specs=in_specs, out_specs=out_specs, check_vma=False
    )
```

time: 91.1 us -> 59 us (0.65); the launches traced: 90.8 us -> 60 us
  between operations: 13.5 us -> 0.15 us
  waiting for transfers between devices: 23.3 us -> 17.3 us
  Pallas kernels: 23.3 us -> 18.3 us
  local copies, waits for them, and re-layouts: 4.85 us -> 0.74 us
  other arithmetic: 1.28 us -> 0.01 us
  starting transfers between devices: 24.5 us -> 23.4 us
    ppermute x14 -> x20, waiting for transfers between devices: 23.3 us -> 17.3 us  [flip(): lax.ppermute(x, axis, [(i, i ^ d) for i in range(lax.axis_size(axis))])]
    pallas_call x5 -> x6, Pallas kernels: 23.3 us -> 18.3 us  [the longest x1 6.82 us: per_device(): pl.pallas_call(functools.partial(product_kernel, sz, [start for start, _...]
    unnamed x22 -> x2, local copies, waits for them, and re-layouts: 4.85 us -> 0.69 us
    convert_element_type x1, other arithmetic: 1.28 us -> 0.01 us  [per_device(): row_notes = jnp.stack([a[-1, :slots] for a in a_parts]).astype(jnp.int32)]
    ppermute x14 -> x20, starting transfers between devices: 24.5 us -> 23.4 us  [flip(): lax.ppermute(x, axis, [(i, i ^ d) for i in range(lax.axis_size(axis))])]
  transfers between devices with their start and end apart: 15 -> 20, of which waited for: 6 -> 6; matrix products, arithmetic and copies ran while one was open for 1% -> 0% of each run, Pallas kernels for 13% -> 24%
where the time goes in v2:
time: 59 us; the launch traced here: 60 us
  starting transfers between devices  23.4 us (40%)
  Pallas kernels  18.3 us (31%)
  waiting for transfers between devices  17.3 us (29%)
  local copies, waits for them, and re-layouts  0.74 us (1%)
    ppermute x20, starting transfers between devices, flip(): lax.ppermute(x, axis, [(i, i ^ d) for i in range(lax.axis_size(axis))])  23.4 us
    ppermute x20, waiting for transfers between devices, flip(): lax.ppermute(x, axis, [(i, i ^ d) for i in range(lax.axis_size(axis))])  17.3 us
    pallas_call x1, Pallas kernels, per_device(): pl.pallas_call(functools.partial(product_kernel, sz, [start for start, _...  6.82 us
    pallas_call x1, Pallas kernels, per_device(): pl.pallas_call(functools.partial(row_meta_kernel, sz), out_shape=[pltpu.S...  4.19 us
    pallas_call x1, Pallas kernels, per_device(): pl.pallas_call(functools.partial(column_meta_kernel, sz), out_shape=[pltp...  2.58 us
    pallas_call x1, Pallas kernels, per_device(): pl.pallas_call(functools.partial(last_kernel, sz), out_shape=[pltpu.VMEM(...  2.28 us
    pallas_call x1, Pallas kernels, per_device(): pl.pallas_call(functools.partial(pack_kernel, sz), out_shape=[pltpu.VMEM(...  1.79 us
  transfers between devices with their start and end apart: 20, of which 6 were waited for; matrix products, arithmetic and copies ran while one was open for 0% of the time, Pallas kernels for 24%

profile of v2, /device:TPU:0, one launch (start us, length us, event | category | flops | bytes accessed | tf_op | source)
XLA Modules:
  0.0 60.0 jit_solution(1978038650258147714)
XLA Ops:
  0.0 1.8 %shard_map.37 = (bf16[528,128]{1,0:T(8,128)(2,1)S(1)}, bf16[528,128]{1,0:T(8,128)(2,1)S(1)}, bf16[528,128]{1,0:T(8,128)(2,1)S(1)}, bf16[528,128]{1,0:T(8,128)(2,...) custom-call(s32[1,24]{1,0:T(1,128)} %pos_row_ref.1, ...), custom_call_target="tpu_custom_call" | custom-call | tf_op jit(solution)/shard_map/pallas_call | solution.py:344
  1.8 3.0 %collective-permute-start = (bf16[3088,128]{1,0:T(8,128)(2,1)S(1)}, bf16[3088,128]{1,0:T(8,128)(2,1)S(1)}, u32[]{:S(2)}, u32[]{:S(2)}) collective-permute-start(bf16[3088,128]{1,0:T(8,128)(2,1)S(1)} %get-tuple-element.50.refs_0_), channel_id=1, source_target_pairs={{0,2},{1,3},{2,0},{3,1},{4,6},{5,7},{6,4},{7,5},{8,10},{9,11},{10,... | collective-permute-start | bytes 2371592 | tf_op jit(solution)/shard_map/ppermute | solution.py:323
  4.8 2.6 %collective-permute-start.4 = (bf16[272,128]{1,0:T(8,128)(2,1)S(1)}, bf16[272,128]{1,0:T(8,128)(2,1)S(1)}, u32[]{:S(2)}, u32[]{:S(2)}) collective-permute-start(bf16[272,128]{1,0:T(8,128)(2,1)S(1)} %get-tuple-element.45), channel_id=1, source_target_pairs={{0,16},{4,20},{8,24},{12,28},{16,0},{20,4},{24,8},{28,12},{1,17},{... | collective-permute-start | bytes 208904 | tf_op jit(solution)/shard_map/ppermute | solution.py:323
  7.4 1.3 %collective-permute-start.5 = (bf16[272,128]{1,0:T(8,128)(2,1)S(1)}, bf16[272,128]{1,0:T(8,128)(2,1)S(1)}, u32[]{:S(2)}, u32[]{:S(2)}) collective-permute-start(bf16[272,128]{1,0:T(8,128)(2,1)S(1)} %get-tuple-element.46), channel_id=1, source_target_pairs={{0,20},{4,16},{8,28},{12,24},{16,4},{20,0},{24,12},{28,8},{1,21},{... | collective-permute-start | bytes 208904 | tf_op jit(solution)/shard_map/ppermute | solution.py:323
  8.7 3.6 %collective-permute-start.6 = (bf16[272,128]{1,0:T(8,128)(2,1)S(1)}, bf16[272,128]{1,0:T(8,128)(2,1)S(1)}, u32[]{:S(2)}, u32[]{:S(2)}) collective-permute-start(bf16[272,128]{1,0:T(8,128)(2,1)S(1)} %get-tuple-element.47), channel_id=1, source_target_pairs={{0,24},{4,28},{8,16},{12,20},{16,8},{20,12},{24,0},{28,4},{1,25},{... | collective-permute-start | bytes 208904 | tf_op jit(solution)/shard_map/ppermute | solution.py:323
  12.3 0.5 collective-permute-start.1
  12.8 0.0 collective-permute-done.4.refs_4_
  12.8 0.3 collective-permute-start.2
  13.1 3.7 %collective-permute-done.5.refs_5_ = bf16[272,128]{1,0:T(8,128)(2,1)S(1)} collective-permute-done((bf16[272,128]{1,0:T(8,128)(2,1)S(1)}, bf16[272,128]{1,0:T(8,128)(2,1)S(1)}, u32[]{:S(2)}, u32[]{:S(2)}) %collective-permute-start.5) | collective-permute-done | bytes 69664 | tf_op jit(solution)/shard_map/ppermute | solution.py:323
  16.8 0.5 collective-permute-start.3
  17.3 0.0 collective-permute-done.6.refs_6_
  17.3 2.6 %collective-permute-start.7 = (bf16[272,128]{1,0:T(8,128)(2,1)S(1)}, bf16[272,128]{1,0:T(8,128)(2,1)S(1)}, u32[]{:S(2)}, u32[]{:S(2)}) collective-permute-start(bf16[272,128]{1,0:T(8,128)(2,1)S(1)} %get-tuple-element.48), channel_id=1, source_target_pairs={{0,28},{4,24},{8,20},{12,16},{16,12},{20,8},{24,4},{28,0},{1,29},{... | collective-permute-start | bytes 208904 | tf_op jit(solution)/shard_map/ppermute | solution.py:323
  20.0 5.9 %collective-permute-done.7.refs_7_ = bf16[272,128]{1,0:T(8,128)(2,1)S(1)} collective-permute-done((bf16[272,128]{1,0:T(8,128)(2,1)S(1)}, bf16[272,128]{1,0:T(8,128)(2,1)S(1)}, u32[]{:S(2)}, u32[]{:S(2)}) %collective-permute-start.7) | collective-permute-done | bytes 69664 | tf_op jit(solution)/shard_map/ppermute | solution.py:323
  25.9 0.0 collective-permute-done.1.refs_1_
  25.9 0.0 collective-permute-done.2.refs_2_
  25.9 0.0 collective-permute-done.3.refs_3_
  25.9 0.7 %shard_map.38 = (bf16[1024,128]{1,0:T(8,128)(2,1)S(1)}, s32[8,24]{1,0:T(8,128)}) custom-call(s32[24]{0:T(128)S(4)} %get-tuple-element.40.plan_ref, bf16[528,128]{1,0:T(8,128)(2,1)S(1)} %get-tuple-element.41.refs_0_, bf16[528,128]{1,0:T(8,128)(2,1)S(1)} %collective-permute-done.1.refs_1_, bf16[528,128]{1,0:T(8,128)(2,1)S(1)} %collective-permute-done.2.refs_2_, ...), custom_call_target="tpu_custom_call" | custom-call | tf_op jit(solution)/shard_map/pallas_call | solution.py:363
  26.6 0.0 collective-permute-done.refs_2_
  26.6 0.0 collective-permute-start.9
  26.6 0.5 collective-permute-start.8
  27.1 0.0 collective-permute-start.11
  27.1 2.3 %collective-permute-start.10 = (bf16[1024,128]{1,0:T(8,128)(2,1)S(1)}, bf16[1024,128]{1,0:T(8,128)(2,1)S(1)}, u32[]{:S(2)}, u32[]{:S(2)}) collective-permute-start(bf16[1024,128]{1,0:T(8,128)(2,1)S(1)} %get-tuple-element.56.refs_0_), channel_id=1, source_target_pairs={{0,16},{4,20},{8,24},{12,28},{16,0},{20,4},{24,8},{28,12},{1,17},{... | collective-permute-start | bytes 786440 | tf_op jit(solution)/shard_map/ppermute | solution.py:323
  29.4 0.2 collective-permute-start.12
  29.6 0.0 copy-start
  29.6 0.7 %copy-done = s32[8,24]{1,0:T(8,128)S(1)} copy-done((s32[8,24]{1,0:T(8,128)S(1)}, s32[8,24]{1,0:T(8,128)}, u32[]{:S(2)}) %copy-start) | copy-done | bytes 792
  30.3 2.6 %shard_map.39 = (s32[64]{0:T(128)S(4)}, bf16[16,128,2048]{2,1,0:T(8,128)(2,1)S(1)}) custom-call(s32[8,24]{1,0:T(8,128)S(1)} %copy-done, s32[16]{0:T(128)S(4)} %get-tuple-element.52.section_ref, s32[24]{0:T(128)S(4)} %get-tuple-element.40.plan_ref), custom_call_target="tpu_custom_call" | custom-call | tf_op jit(solution)/shard_map/pallas_call | solution.py:374
  32.9 0.0 collective-permute-done.9.refs_3_
  32.9 0.0 collective-permute-done.8.refs_1_
  33.0 4.2 %shard_map.40 = (s32[136]{0:T(256)S(4)}, s32[258]{0:T(512)S(4)}, bf16[128,128,128]{2,1,0:T(8,128)(2,1)S(1)}) custom-call(s32[4,24]{1,0:T(4,128)S(1)} %maximum_convert_fusion.notes_ref, s32[16]{0:T(128)S(4)} %get-tuple-element.52.section_ref, s32[64]{0:T(128)S(4)} %get-tuple-element.54.b_list, bf16[3088,128]{1,0:T(8,128)(2,1)S(1)} %get-tuple-element.50.refs_0_, ...), custom_call_target="tpu_custom_call" | custom-call | tf_op jit(solution)/shard_map/pallas_call | solution.py:395
  37.2 2.9 %collective-permute-done.11.refs_2_ = bf16[1024,128]{1,0:T(8,128)(2,1)S(1)} collective-permute-done((bf16[1024,128]{1,0:T(8,128)(2,1)S(1)}, bf16[1024,128]{1,0:T(8,128)(2,1)S(1)}, u32[]{:S(2)}, u32[]{:S(2)}) %collective-permute-start.11) | collective-permute-done | bytes 262176 | tf_op jit(solution)/shard_map/ppermute | solution.py:323
  40.1 1.0 %collective-permute-start.14 = (bf16[1024,128]{1,0:T(8,128)(2,1)S(1)}, bf16[1024,128]{1,0:T(8,128)(2,1)S(1)}, u32[]{:S(2)}, u32[]{:S(2)}) collective-permute-start(bf16[1024,128]{1,0:T(8,128)(2,1)S(1)} %collective-permute-done.11.refs_2_), channel_id=1, source_target_pairs={{0,4},{4,0},{8,12},{12,8},{16,20},{20,16},{24,28},{28,24},{1,5},{5... | collective-permute-start | bytes 786440 | tf_op jit(solution)/shard_map/ppermute | solution.py:323
  41.1 0.8 %collective-permute-done.10.refs_4_ = bf16[1024,128]{1,0:T(8,128)(2,1)S(1)} collective-permute-done((bf16[1024,128]{1,0:T(8,128)(2,1)S(1)}, bf16[1024,128]{1,0:T(8,128)(2,1)S(1)}, u32[]{:S(2)}, u32[]{:S(2)}) %collective-permute-start.10) | collective-permute-done | bytes 262176 | tf_op jit(solution)/shard_map/ppermute | solution.py:323
  41.9 0.0 collective-permute-done.12.refs_1_
  41.9 0.1 collective-permute-start.15
  42.0 2.0 %collective-permute-start.13 = (bf16[512,128]{1,0:T(8,128)(2,1)S(1)}, bf16[512,128]{1,0:T(8,128)(2,1)S(1)}, u32[]{:S(2)}, u32[]{:S(2)}) collective-permute-start(bf16[512,128]{1,0:T(8,128)(2,1)S(1)} %get-tuple-element.74), channel_id=1, source_target_pairs={{0,8},{4,12},{8,0},{12,4},{16,24},{20,28},{24,16},{28,20},{1,9},{5... | collective-permute-start | bytes 393224 | tf_op jit(solution)/shard_map/ppermute | solution.py:323
  44.0 0.6 collective-permute-start.16
  44.6 0.8 %collective-permute-start.17 = (bf16[512,128]{1,0:T(8,128)(2,1)S(1)}, bf16[512,128]{1,0:T(8,128)(2,1)S(1)}, u32[]{:S(2)}, u32[]{:S(2)}) collective-permute-start(bf16[512,128]{1,0:T(8,128)(2,1)S(1)} %slice.28), channel_id=1, source_target_pairs={{0,16},{4,20},{8,24},{12,28},{16,0},{20,4},{24,8},{28,12},{1,17},{... | collective-permute-start | bytes 393224 | tf_op jit(solution)/shard_map/ppermute | solution.py:323
  45.5 2.9 %collective-permute-done.15.refs_5_ = bf16[512,128]{1,0:T(8,128)(2,1)S(1)} collective-permute-done((bf16[512,128]{1,0:T(8,128)(2,1)S(1)}, bf16[512,128]{1,0:T(8,128)(2,1)S(1)}, u32[]{:S(2)}, u32[]{:S(2)}) %collective-permute-start.15) | collective-permute-done | bytes 131104 | tf_op jit(solution)/shard_map/ppermute | solution.py:323
  48.4 1.0 %collective-permute-start.18 = (bf16[512,128]{1,0:T(8,128)(2,1)S(1)}, bf16[512,128]{1,0:T(8,128)(2,1)S(1)}, u32[]{:S(2)}, u32[]{:S(2)}) collective-permute-start(bf16[512,128]{1,0:T(8,128)(2,1)S(1)} %collective-permute-done.15.refs_5_), channel_id=1, source_target_pairs={{0,4},{4,0},{8,12},{12,8},{16,20},{20,16},{24,28},{28,24},{1,5},{5... | collective-permute-start | bytes 393224 | tf_op jit(solution)/shard_map/ppermute | solution.py:323
  49.3 1.0 %collective-permute-done.13.refs_6_ = bf16[512,128]{1,0:T(8,128)(2,1)S(1)} collective-permute-done((bf16[512,128]{1,0:T(8,128)(2,1)S(1)}, bf16[512,128]{1,0:T(8,128)(2,1)S(1)}, u32[]{:S(2)}, u32[]{:S(2)}) %collective-permute-start.13) | collective-permute-done | bytes 131104 | tf_op jit(solution)/shard_map/ppermute | solution.py:323
  50.4 0.0 collective-permute-done.14.refs_3_
  50.4 0.5 collective-permute-start.19
  50.9 6.8 %shard_map.41 = (f32[1024,2048]{1,0:T(8,128)S(1)}, f32[1024,2048]{1,0:T(8,128)}, bf16[16,128,2048]{2,1,0:T(8,128)(2,1)S(1)}) custom-call(s32[136]{0:T(256)S(4)} %get-tuple-element.62.a_list, s32[64]{0:T(128)S(4)} %get-tuple-element.54.b_list, bf16[16,128,2048]{2,1,0:T(8,128)(2,1)S(1)} %get-tuple-element.63.b_clear, ...), custom_call_target="tpu_custom_call", output_to_operand_aliasing={{2}: (2, {})} | custom-call | flops 2000000000 | bytes 12582912 | tf_op jit(solution)/shard_map/pallas_call | solution.py:436
  57.7 0.0 collective-permute-done.16.refs_0_
  57.7 0.0 collective-permute-done.17.refs_1_
  57.7 0.0 collective-permute-done.18.refs_2_
  57.7 0.0 collective-permute-done.19.refs_3_
  57.7 2.3 %shard_map.42 = (f32[1024,2048]{1,0:T(8,128)S(1)}, f32[1024,2048]{1,0:T(8,128)}) custom-call(s32[258]{0:T(512)S(4)} %get-tuple-element.55.late_list, f32[1024,2048]{1,0:T(8,128)S(1)} %get-tuple-element.70.total_in, f32[1024,2048]{1,0:T(8,128)} %get-tuple-element.71.out_in, ...), custom_call_target="tpu_custom_call", output_to_operand_aliasing={{0}: (1, {}), {1}: (2, {})} | custom-call | tf_op jit(solution)/shard_map/pallas_call | solution.py:450
  (7 shorter events, 0.1 us)
Async XLA Ops:
  1.8 24.8 %collective-permute-start = (bf16[3088,128]{1,0:T(8,128)(2,1)S(1)}, bf16[3088,128]{1,0:T(8,128)(2,1)S(1)}, u32[]{:S(2)}, u32[]{:S(2)}) collective-permute-start(bf16[3088,128]{1,0:T(8,128)(2,1)S(1)} %get-tuple-element.50.refs_0_), channel_id=1, source_target_pairs={{0,2},{1,3},{2,0},{3,1},{4,6},{5,7},{6,4},{7,5},{8,10},{9,11},{10,... | collective-permute-start | bytes 2371592 | tf_op jit(solution)/shard_map/ppermute | solution.py:323
  4.8 8.0 %collective-permute-start.4 = (bf16[272,128]{1,0:T(8,128)(2,1)S(1)}, bf16[272,128]{1,0:T(8,128)(2,1)S(1)}, u32[]{:S(2)}, u32[]{:S(2)}) collective-permute-start(bf16[272,128]{1,0:T(8,128)(2,1)S(1)} %get-tuple-element.45), channel_id=1, source_target_pairs={{0,16},{4,20},{8,24},{12,28},{16,0},{20,4},{24,8},{28,12},{1,17},{... | collective-permute-start | bytes 208904 | tf_op jit(solution)/shard_map/ppermute | solution.py:323
  7.4 9.4 %collective-permute-start.5 = (bf16[272,128]{1,0:T(8,128)(2,1)S(1)}, bf16[272,128]{1,0:T(8,128)(2,1)S(1)}, u32[]{:S(2)}, u32[]{:S(2)}) collective-permute-start(bf16[272,128]{1,0:T(8,128)(2,1)S(1)} %get-tuple-element.46), channel_id=1, source_target_pairs={{0,20},{4,16},{8,28},{12,24},{16,4},{20,0},{24,12},{28,8},{1,21},{... | collective-permute-start | bytes 208904 | tf_op jit(solution)/shard_map/ppermute | solution.py:323
  8.7 8.7 %collective-permute-start.6 = (bf16[272,128]{1,0:T(8,128)(2,1)S(1)}, bf16[272,128]{1,0:T(8,128)(2,1)S(1)}, u32[]{:S(2)}, u32[]{:S(2)}) collective-permute-start(bf16[272,128]{1,0:T(8,128)(2,1)S(1)} %get-tuple-element.47), channel_id=1, source_target_pairs={{0,24},{4,28},{8,16},{12,20},{16,8},{20,12},{24,0},{28,4},{1,25},{... | collective-permute-start | bytes 208904 | tf_op jit(solution)/shard_map/ppermute | solution.py:323
  12.3 13.6 %collective-permute-start.1 = (bf16[528,128]{1,0:T(8,128)(2,1)S(1)}, bf16[528,128]{1,0:T(8,128)(2,1)S(1)}, u32[]{:S(2)}, u32[]{:S(2)}) collective-permute-start(bf16[528,128]{1,0:T(8,128)(2,1)S(1)} %get-tuple-element.42), channel_id=1, source_target_pairs={{0,4},{4,0},{8,12},{12,8},{16,20},{20,16},{24,28},{28,24},{1,5},{5... | collective-permute-start | bytes 405512 | tf_op jit(solution)/shard_map/ppermute | solution.py:323
  12.8 13.1 %collective-permute-start.2 = (bf16[528,128]{1,0:T(8,128)(2,1)S(1)}, bf16[528,128]{1,0:T(8,128)(2,1)S(1)}, u32[]{:S(2)}, u32[]{:S(2)}) collective-permute-start(bf16[528,128]{1,0:T(8,128)(2,1)S(1)} %get-tuple-element.43), channel_id=1, source_target_pairs={{0,8},{4,12},{8,0},{12,4},{16,24},{20,28},{24,16},{28,20},{1,9},{5... | collective-permute-start | bytes 405512 | tf_op jit(solution)/shard_map/ppermute | solution.py:323
  16.8 9.1 %collective-permute-start.3 = (bf16[528,128]{1,0:T(8,128)(2,1)S(1)}, bf16[528,128]{1,0:T(8,128)(2,1)S(1)}, u32[]{:S(2)}, u32[]{:S(2)}) collective-permute-start(bf16[528,128]{1,0:T(8,128)(2,1)S(1)} %get-tuple-element.44), channel_id=1, source_target_pairs={{0,12},{4,8},{8,4},{12,0},{16,28},{20,24},{24,20},{28,16},{1,13},{... | collective-permute-start | bytes 405512 | tf_op jit(solution)/shard_map/ppermute | solution.py:323
  17.3 8.5 %collective-permute-start.7 = (bf16[272,128]{1,0:T(8,128)(2,1)S(1)}, bf16[272,128]{1,0:T(8,128)(2,1)S(1)}, u32[]{:S(2)}, u32[]{:S(2)}) collective-permute-start(bf16[272,128]{1,0:T(8,128)(2,1)S(1)} %get-tuple-element.48), channel_id=1, source_target_pairs={{0,28},{4,24},{8,20},{12,16},{16,12},{20,8},{24,4},{28,0},{1,29},{... | collective-permute-start | bytes 208904 | tf_op jit(solution)/shard_map/ppermute | solution.py:323
  26.6 6.3 %collective-permute-start.9 = (bf16[3088,128]{1,0:T(8,128)(2,1)S(1)}, bf16[3088,128]{1,0:T(8,128)(2,1)S(1)}, u32[]{:S(2)}, u32[]{:S(2)}) collective-permute-start(bf16[3088,128]{1,0:T(8,128)(2,1)S(1)} %collective-permute-done.refs_2_), channel_id=1, source_target_pairs={{0,1},{1,0},{2,3},{3,2},{4,5},{5,4},{6,7},{7,6},{8,9},{9,8},{10,11... | collective-permute-start | bytes 2371592 | tf_op jit(solution)/shard_map/ppermute | solution.py:323
  26.6 6.3 %collective-permute-start.8 = (bf16[3088,128]{1,0:T(8,128)(2,1)S(1)}, bf16[3088,128]{1,0:T(8,128)(2,1)S(1)}, u32[]{:S(2)}, u32[]{:S(2)}) collective-permute-start(bf16[3088,128]{1,0:T(8,128)(2,1)S(1)} %get-tuple-element.50.refs_0_), channel_id=1, source_target_pairs={{0,1},{1,0},{2,3},{3,2},{4,5},{5,4},{6,7},{7,6},{8,9},{9,8},{10,11... | collective-permute-start | bytes 2371592 | tf_op jit(solution)/shard_map/ppermute | solution.py:323
  27.1 13.0 %collective-permute-start.11 = (bf16[1024,128]{1,0:T(8,128)(2,1)S(1)}, bf16[1024,128]{1,0:T(8,128)(2,1)S(1)}, u32[]{:S(2)}, u32[]{:S(2)}) collective-permute-start(bf16[1024,128]{1,0:T(8,128)(2,1)S(1)} %get-tuple-element.56.refs_0_), channel_id=1, source_target_pairs={{0,8},{4,12},{8,0},{12,4},{16,24},{20,28},{24,16},{28,20},{1,9},{5... | collective-permute-start | bytes 786440 | tf_op jit(solution)/shard_map/ppermute | solution.py:323
  27.1 14.8 %collective-permute-start.10 = (bf16[1024,128]{1,0:T(8,128)(2,1)S(1)}, bf16[1024,128]{1,0:T(8,128)(2,1)S(1)}, u32[]{:S(2)}, u32[]{:S(2)}) collective-permute-start(bf16[1024,128]{1,0:T(8,128)(2,1)S(1)} %get-tuple-element.56.refs_0_), channel_id=1, source_target_pairs={{0,16},{4,20},{8,24},{12,28},{16,0},{20,4},{24,8},{28,12},{1,17},{... | collective-permute-start | bytes 786440 | tf_op jit(solution)/shard_map/ppermute | solution.py:323
  29.4 12.5 %collective-permute-start.12 = (bf16[1024,128]{1,0:T(8,128)(2,1)S(1)}, bf16[1024,128]{1,0:T(8,128)(2,1)S(1)}, u32[]{:S(2)}, u32[]{:S(2)}) collective-permute-start(bf16[1024,128]{1,0:T(8,128)(2,1)S(1)} %get-tuple-element.56.refs_0_), channel_id=1, source_target_pairs={{0,4},{4,0},{8,12},{12,8},{16,20},{20,16},{24,28},{28,24},{1,5},{5... | collective-permute-start | bytes 786440 | tf_op jit(solution)/shard_map/ppermute | solution.py:323
  29.6 0.7 %copy-start = (s32[8,24]{1,0:T(8,128)S(1)}, s32[8,24]{1,0:T(8,128)}, u32[]{:S(2)}) copy-start(s32[8,24]{1,0:T(8,128)} %get-tuple-element.53.notes_ref) | copy-start | bytes 2308
  40.1 10.3 %collective-permute-start.14 = (bf16[1024,128]{1,0:T(8,128)(2,1)S(1)}, bf16[1024,128]{1,0:T(8,128)(2,1)S(1)}, u32[]{:S(2)}, u32[]{:S(2)}) collective-permute-start(bf16[1024,128]{1,0:T(8,128)(2,1)S(1)} %collective-permute-done.11.refs_2_), channel_id=1, source_target_pairs={{0,4},{4,0},{8,12},{12,8},{16,20},{20,16},{24,28},{28,24},{1,5},{5... | collective-permute-start | bytes 786440 | tf_op jit(solution)/shard_map/ppermute | solution.py:323
  41.9 6.4 %collective-permute-start.15 = (bf16[512,128]{1,0:T(8,128)(2,1)S(1)}, bf16[512,128]{1,0:T(8,128)(2,1)S(1)}, u32[]{:S(2)}, u32[]{:S(2)}) collective-permute-start(bf16[512,128]{1,0:T(8,128)(2,1)S(1)} %get-tuple-element.73), channel_id=1, source_target_pairs={{0,8},{4,12},{8,0},{12,4},{16,24},{20,28},{24,16},{28,20},{1,9},{5... | collective-permute-start | bytes 393224 | tf_op jit(solution)/shard_map/ppermute | solution.py:323
  42.0 8.4 %collective-permute-start.13 = (bf16[512,128]{1,0:T(8,128)(2,1)S(1)}, bf16[512,128]{1,0:T(8,128)(2,1)S(1)}, u32[]{:S(2)}, u32[]{:S(2)}) collective-permute-start(bf16[512,128]{1,0:T(8,128)(2,1)S(1)} %get-tuple-element.74), channel_id=1, source_target_pairs={{0,8},{4,12},{8,0},{12,4},{16,24},{20,28},{24,16},{28,20},{1,9},{5... | collective-permute-start | bytes 393224 | tf_op jit(solution)/shard_map/ppermute | solution.py:323
  44.0 13.7 %collective-permute-start.16 = (bf16[512,128]{1,0:T(8,128)(2,1)S(1)}, bf16[512,128]{1,0:T(8,128)(2,1)S(1)}, u32[]{:S(2)}, u32[]{:S(2)}) collective-permute-start(bf16[512,128]{1,0:T(8,128)(2,1)S(1)} %get-tuple-element.73), channel_id=1, source_target_pairs={{0,4},{4,0},{8,12},{12,8},{16,20},{20,16},{24,28},{28,24},{1,5},{5... | collective-permute-start | bytes 393224 | tf_op jit(solution)/shard_map/ppermute | solution.py:323
  44.6 13.1 %collective-permute-start.17 = (bf16[512,128]{1,0:T(8,128)(2,1)S(1)}, bf16[512,128]{1,0:T(8,128)(2,1)S(1)}, u32[]{:S(2)}, u32[]{:S(2)}) collective-permute-start(bf16[512,128]{1,0:T(8,128)(2,1)S(1)} %slice.28), channel_id=1, source_target_pairs={{0,16},{4,20},{8,24},{12,28},{16,0},{20,4},{24,8},{28,12},{1,17},{... | collective-permute-start | bytes 393224 | tf_op jit(solution)/shard_map/ppermute | solution.py:323
  48.4 9.3 %collective-permute-start.18 = (bf16[512,128]{1,0:T(8,128)(2,1)S(1)}, bf16[512,128]{1,0:T(8,128)(2,1)S(1)}, u32[]{:S(2)}, u32[]{:S(2)}) collective-permute-start(bf16[512,128]{1,0:T(8,128)(2,1)S(1)} %collective-permute-done.15.refs_5_), channel_id=1, source_target_pairs={{0,4},{4,0},{8,12},{12,8},{16,20},{20,16},{24,28},{28,24},{1,5},{5... | collective-permute-start | bytes 393224 | tf_op jit(solution)/shard_map/ppermute | solution.py:323
  50.4 7.3 %collective-permute-start.19 = (bf16[512,128]{1,0:T(8,128)(2,1)S(1)}, bf16[512,128]{1,0:T(8,128)(2,1)S(1)}, u32[]{:S(2)}, u32[]{:S(2)}) collective-permute-start(bf16[512,128]{1,0:T(8,128)(2,1)S(1)} %collective-permute-done.13.refs_6_), channel_id=1, source_target_pairs={{0,4},{4,0},{8,12},{12,8},{16,20},{20,16},{24,28},{28,24},{1,5},{5... | collective-permute-start | bytes 393224 | tf_op jit(solution)/shard_map/ppermute | solution.py:323
